TPU v7x, 256 devices: a whole 4x4x8 slice. The times are simulated.
256 devices in a mesh: doc: 16 (over x_hi, z), hidden: 16 (over y, x_lo, core).
Axes of the slice: x: 4 (x_hi: 2, x_lo: 2; x = x_hi * 2 + x_lo), y: 4, z: 8, core: 2. Of those that a mesh axis runs over, the one named last changes fastest.
Arguments:
- train_acts: bfloat16 [12288, 28672], P('doc', 'hidden'), may hold values from -0.4375 to 0.4375
- train_grads: bfloat16 [12288, 8192], P('doc', 'hidden'), may hold values from -0.625 to 0.625
- query_acts: bfloat16 [8192, 28672], P('doc', 'hidden'), may hold values from -0.4375 to 0.4375
- query_grads: bfloat16 [8192, 8192], P('doc', 'hidden'), may hold values from -0.625 to 0.625
- train_seg: int32 [16, 768], P('doc'), may hold values from 0 to 7, never falling along the last dimension, each value on 1 to 192 neighbouring positions
- query_seg: int32 [16, 512], replicated, may hold values from 0 to 7, never falling along the last dimension, each value on 1 to 128 neighbouring positions
Outputs:
- influence: float32 [128, 32], P('doc')
All inputs are finite; a program needn't handle non-finite values.
Results may differ from a plain program's by a relative error of at most 0.0003.
Values may be sent and summed in bfloat16 or wider, within the bound.
A program may use at most 64 MiB of HBM per device.

v0:
```python
import math

import jax
import jax.numpy as jnp
from jax import lax
from jax.sharding import PartitionSpec as P

ST = 8
SQ = 8
CYCLE = 4


def from_behind(value, axis, by):
    devices = lax.axis_size(axis)
    return lax.ppermute(value, axis, [(i, (i + by) % devices) for i in range(devices)])


def on_device(train_acts, train_grads, query_acts, query_grads, train_seg, query_seg):
    rows = train_acts.shape[0]
    width_q = query_acts.shape[0]
    groups = lax.axis_size("hidden")
    share = rows // groups
    circle_size = lax.axis_size("doc")
    position = lax.axis_index("doc")
    place = lax.axis_index("hidden")
    factor = math.sqrt(ST * SQ / (rows * width_q))
    train_ids = jnp.arange(ST, dtype=jnp.int32)
    query_ids = jnp.arange(SQ, dtype=jnp.int32)
    contract = (((1,), (1,)), ((), ()))

    def tally(block, step):
        cols_a, cols_g = block
        owner = (position - step) % circle_size
        seg_query = lax.dynamic_index_in_dim(query_seg, owner, 0, keepdims=False)
        act_gram = lax.dot_general(train_acts, cols_a, contract, preferred_element_type=jnp.float32)
        grad_gram = lax.dot_general(
            train_grads, cols_g, contract, preferred_element_type=jnp.float32
        )
        summed = lax.psum_scatter(
            jnp.concatenate([act_gram, grad_gram], axis=1),
            "hidden",
            scatter_dimension=0,
            tiled=True,
        )
        pair = summed[:, :width_q] * summed[:, width_q:]
        seg_here = lax.dynamic_slice_in_dim(train_seg[0], place * share, share)
        onehot_train = (train_ids[:, None] == seg_here[None, :]).astype(jnp.float32)
        onehot_query = (seg_query[:, None] == query_ids[None, :]).astype(jnp.float32)
        left = jnp.dot(onehot_train, pair, precision=lax.Precision.HIGHEST)
        return jnp.dot(left, onehot_query, precision=lax.Precision.HIGHEST) * factor

    blocks = [(query_acts, query_grads)]
    current = (query_acts, query_grads)
    for step in range(1, CYCLE):
        current = from_behind((current[0], current[1]), "doc", 1)
        blocks.append(current)
    partials = [tally(blocks[step], step) for step in range(CYCLE)]
    totals = [lax.psum(part, "hidden") for part in partials]
    return jnp.concatenate(totals, axis=1)


def solution(mesh):
    in_specs = (
        P("doc", "hidden"),
        P("doc", "hidden"),
        P("doc", "hidden"),
        P("doc", "hidden"),
        P("doc", None),
        P(),
    )
    out_specs = P("doc", None)
    return jax.shard_map(
        on_device, mesh=mesh, in_specs=in_specs, out_specs=out_specs, check_vma=False
    )
```

profile of v0, /device:TPU:1, one launch (start us, length us, event | category | flops | bytes accessed | tf_op | source)
XLA Modules:
  0.0 499.7 jit_solution(10629320670066512416)
XLA Ops:
  6.5 2.0 fusion.22
  9.3 1.6 fusion.21
  10.9 1.9 pad_maximum_fusion
  12.8 3.5 copy.7
  16.4 2.5 collective-permute-start
  18.9 1.6 collective-permute-start.1
  20.6 56.0 %collective-permute-done.1 = bf16[512,512]{1,0:T(8,128)(2,1)S(1)} collective-permute-done((bf16[512,512]{1,0:T(8,128)(2,1)}, bf16[512,512]{1,0:T(8,128)(2,1)S(1)}, u32[]{:S(2)}, u32[]{:S(2)}) %collective-permute-start.1) | collective-permute-done | bytes 524320 | tf_op jit(solution)/shard_map/ppermute | solution.py:15
  78.6 1.6 fusion.23
  80.2 1.9 pad_maximum_fusion.1
  82.1 3.6 copy.9
  86.0 55.2 %collective-permute-done.3 = bf16[512,512]{1,0:T(8,128)(2,1)S(1)} collective-permute-done((bf16[512,512]{1,0:T(8,128)(2,1)}, bf16[512,512]{1,0:T(8,128)(2,1)S(1)}, u32[]{:S(2)}, u32[]{:S(2)}) %collective-permute-start.3) | collective-permute-done | bytes 524320 | tf_op jit(solution)/shard_map/ppermute | solution.py:15
  142.1 1.3 copy-done.5
  143.3 1.6 fusion.25
  144.9 1.9 pad_maximum_fusion.2
  146.8 3.6 copy.11
  150.9 54.1 %collective-permute-done.5 = bf16[512,512]{1,0:T(8,128)(2,1)S(1)} collective-permute-done((bf16[512,512]{1,0:T(8,128)(2,1)}, bf16[512,512]{1,0:T(8,128)(2,1)S(1)}, u32[]{:S(2)}, u32[]{:S(2)}) %collective-permute-start.5) | collective-permute-done | bytes 524320 | tf_op jit(solution)/shard_map/ppermute | solution.py:15
  205.6 1.6 fusion.27
  207.2 1.8 pad_maximum_fusion.3
  209.1 3.5 copy.13
  214.3 16.2 %reduce-scatter.13.cloned.1.call-done = f32[48,1024]{1,0:T(8,128)} async-done(((f32[768,1024]{1,0:T(8,128)}), f32[48,1024]{1,0:T(8,128)}) %reduce-scatter.13.cloned.1.call-update) | async-done | bytes 196624
  232.3 63.3 %reduce-scatter.15.cloned.1.call-done = f32[48,1024]{1,0:T(8,128)} async-done(((f32[768,1024]{1,0:T(8,128)}), f32[48,1024]{1,0:T(8,128)}) %reduce-scatter.15.cloned.1.call-update) | async-done | bytes 196624
  297.4 69.7 %reduce-scatter.17.cloned.1.call-done = f32[48,1024]{1,0:T(8,128)} async-done(((f32[768,1024]{1,0:T(8,128)}), f32[48,1024]{1,0:T(8,128)}) %reduce-scatter.17.cloned.1.call-update) | async-done | bytes 196624
  368.9 68.7 %reduce-scatter.19.cloned.1.call-done = f32[48,1024]{1,0:T(8,128)} async-done(((f32[768,1024]{1,0:T(8,128)}), f32[48,1024]{1,0:T(8,128)}) %reduce-scatter.19.cloned.1.call-update) | async-done | bytes 196624
  439.3 53.1 %all-reduce = (f32[8,8]{1,0:T(8,128)S(1)}, f32[8,8]{1,0:T(8,128)S(1)}, f32[8,8]{1,0:T(8,128)S(1)}, f32[8,8]{1,0:T(8,128)S(1)}) all-reduce(f32[8,8]{1,0:T(8,128)S(1)} %convolution_multiply_fusion, f32[8,8]{1,0:T(8,128)S(1)} %convolution_multiply_fusion.1, ...), channel_id=1, replica_groups=mesh['doc'=16,'hidden'=16] {'hidden'}, use_global_device_ids=true, to_apply=%region_7.8 | all-reduce | flops 256 | bytes 2048 | tf_op jit(solution)/shard_map/psum | solution.py:58
  (54 shorter events, 14.1 us)
Async XLA Ops:
  6.5 2.2 copy-start
  6.5 224.0 %reduce-scatter.13.cloned.1.call-start = ((), (), s32[]{:S(2)}) async-start(), calls=%async_computation.4 | async-start | bytes 3342336
  6.5 2.7 copy-start.4
  16.3 60.3 %copy-start.1 = (bf16[768,512]{1,0:T(8,128)(2,1)S(1)}, bf16[768,512]{1,0:T(8,128)(2,1)}, u32[]{:S(2)}) copy-start(bf16[768,512]{1,0:T(8,128)(2,1)} %param.7) | copy-start | bytes 2359300
  16.3 279.3 %reduce-scatter.15.cloned.1.call-start = ((), (), s32[]{:S(2)}) async-start(), calls=%async_computation.5 | async-start | bytes 3342336
  16.4 61.0 %collective-permute-start = (bf16[512,1792]{1,0:T(8,128)(2,1)}, bf16[512,1792]{1,0:T(8,128)(2,1)S(1)}, u32[]{:S(2)}, u32[]{:S(2)}) collective-permute-start(bf16[512,1792]{1,0:T(8,128)(2,1)} %param.8), channel_id=1, source_target_pairs={{0,16},{16,32},{32,48},{48,64},{64,80},{80,96},{96,112},{112,128},... | collective-permute-start | bytes 5505032 | tf_op jit(solution)/shard_map/ppermute | solution.py:15
  18.9 57.6 %collective-permute-start.1 = (bf16[512,512]{1,0:T(8,128)(2,1)}, bf16[512,512]{1,0:T(8,128)(2,1)S(1)}, u32[]{:S(2)}, u32[]{:S(2)}) collective-permute-start(bf16[512,512]{1,0:T(8,128)(2,1)} %param.9), channel_id=1, source_target_pairs={{0,16},{16,32},{32,48},{48,64},{64,80},{80,96},{96,112},{112,128},... | collective-permute-start | bytes 1572872 | tf_op jit(solution)/shard_map/ppermute | solution.py:15
  76.6 0.8 copy-start.3
  77.4 1.2 copy-start.6
  85.8 281.4 %reduce-scatter.17.cloned.1.call-start = ((), (), s32[]{:S(2)}) async-start(), calls=%async_computation.6 | async-start | bytes 3342336
  85.8 56.3 %collective-permute-start.2 = (bf16[512,1792]{1,0:T(8,128)(2,1)}, bf16[512,1792]{1,0:T(8,128)(2,1)S(1)}, u32[]{:S(2)}, u32[]{:S(2)}) collective-permute-start(bf16[512,1792]{1,0:T(8,128)(2,1)} %copy-done.6), channel_id=1, source_target_pairs={{0,16},{16,32},{32,48},{48,64},{64,80},{80,96},{96,112},{112,128},... | collective-permute-start | bytes 5505032 | tf_op jit(solution)/shard_map/ppermute | solution.py:15
  85.9 55.3 %collective-permute-start.3 = (bf16[512,512]{1,0:T(8,128)(2,1)}, bf16[512,512]{1,0:T(8,128)(2,1)S(1)}, u32[]{:S(2)}, u32[]{:S(2)}) collective-permute-start(bf16[512,512]{1,0:T(8,128)(2,1)} %copy-done.3), channel_id=1, source_target_pairs={{0,16},{16,32},{32,48},{48,64},{64,80},{80,96},{96,112},{112,128},... | collective-permute-start | bytes 1572872 | tf_op jit(solution)/shard_map/ppermute | solution.py:15
  141.2 0.8 copy-start.2
  142.1 1.3 copy-start.5
  150.5 287.1 %reduce-scatter.19.cloned.1.call-start = ((), (), s32[]{:S(2)}) async-start(), calls=%async_computation.7 | async-start | bytes 3342336
  150.5 55.1 %collective-permute-start.4 = (bf16[512,1792]{1,0:T(8,128)(2,1)}, bf16[512,1792]{1,0:T(8,128)(2,1)S(1)}, u32[]{:S(2)}, u32[]{:S(2)}) collective-permute-start(bf16[512,1792]{1,0:T(8,128)(2,1)} %copy-done.5), channel_id=1, source_target_pairs={{0,16},{16,32},{32,48},{48,64},{64,80},{80,96},{96,112},{112,128},... | collective-permute-start | bytes 5505032 | tf_op jit(solution)/shard_map/ppermute | solution.py:15
  150.6 54.4 %collective-permute-start.5 = (bf16[512,512]{1,0:T(8,128)(2,1)}, bf16[512,512]{1,0:T(8,128)(2,1)S(1)}, u32[]{:S(2)}, u32[]{:S(2)}) collective-permute-start(bf16[512,512]{1,0:T(8,128)(2,1)} %copy-done.2), channel_id=1, source_target_pairs={{0,16},{16,32},{32,48},{48,64},{64,80},{80,96},{96,112},{112,128},... | collective-permute-start | bytes 1572872 | tf_op jit(solution)/shard_map/ppermute | solution.py:15
Sparse Core Ops, SparseCore 0:
  16.5 214.0 reduce-scatter.12
  233.1 62.5 reduce-scatter.14
  298.2 68.8 reduce-scatter.16
  369.5 67.9 reduce-scatter.18
where the time goes:
time: 502 us; the launch traced here: 500 us
  waiting for transfers between devices  383 us (76%)
  blocking collectives  53.1 us (11%)
  local copies, waits for them, and re-layouts  24.3 us (5%)
  between operations  13.4 us (3%)
  matrix products  12.5 us (2%)
  other arithmetic  8.18 us (2%)
    unnamed x8, waiting for transfers between devices  218 us
    ppermute x6, waiting for transfers between devices, from_behind(): lax.ppermute(value, axis, [(i, (i + by) % devices) for i in range(devices)])  165 us
    psum x1, blocking collectives, on_device(): totals = [lax.psum(part, 'hidden') for part in partials]  53.1 us
    unnamed x26, local copies, waits for them, and re-layouts  18.9 us
  transfers between devices with their start and end apart: 10, of which 7 were waited for; matrix products, arithmetic and copies ran while one was open for 6% of the time, Pallas kernels for 0%

commit v1 on v0

v1 whole, which is shorter than its diff:
```python
import functools
import math

import jax
import jax.numpy as jnp
from jax import lax
from jax.experimental import pallas as pl
from jax.experimental.pallas import tpu as pltpu
from jax.sharding import PartitionSpec as P

ST = 8
SQ = 8
CYCLE = 4
NY = 4
NX = 2
NCORE = 2
CHUNKS = 4
TPARTS = 4
LANES = 128
MESH = pl.DeviceIdType.MESH
CONTRACT = (((1,), (1,)), ((), ()))


def kernel(
    n_doc,
    ta_hbm,
    tg_hbm,
    qa_hbm,
    qg_hbm,
    tseg_ref,
    qseg_ref,
    out_ref,
    tbuf,
    qbuf,
    gram,
    yrecv,
    xsend,
    xrecv,
    pairs,
    segn,
    fin,
    local_sem,
    own_send,
    own_recv,
    z1_send,
    z1_recv,
    z2_send,
    z2_recv,
    tz_send,
    tz_recv,
    tf_send,
    tf_recv,
    y_send,
    y_recv,
    x_send,
    x_recv,
    f_send,
    f_recv,
):
    rows_t, wide_a = ta_hbm.shape
    rows_q, wide_g = qg_hbm.shape
    half = rows_q // NCORE
    chunk = half // CHUNKS
    part = rows_t // TPARTS
    ry = chunk // NY
    lx = rows_t // NX
    factor = math.sqrt(ST * SQ / (rows_t * rows_q))

    doc = lax.axis_index("doc")
    place = lax.axis_index("hidden")
    core = lax.rem(place, NCORE)
    other = 1 - core
    my_x = lax.rem(place // NCORE, NX)
    my_y = place // (NCORE * NX)
    plane = place - core
    up = lax.rem(doc + 1, n_doc)
    down = lax.rem(doc + n_doc - 1, n_doc)
    sibling = (doc, plane + other)
    x_peer = (doc, my_y * (NX * NCORE) + (1 - my_x) * NCORE + core)

    def y_of(d):
        return lax.rem(my_y + d, NY)

    def y_peer(d):
        return (doc, y_of(d) * (NX * NCORE) + my_x * NCORE + core)

    greet = [sibling, (up, place), (up, plane + other), (down, place), (down, plane + other), x_peer]
    greet += [y_peer(d) for d in range(1, NY)]
    barrier = pltpu.get_barrier_semaphore()
    for who in greet:
        pl.semaphore_signal(barrier, inc=1, device_id=who, device_id_type=MESH)
    pl.semaphore_wait(barrier, len(greet))

    def remote(src, dst, send, recv, who):
        return pltpu.make_async_remote_copy(
            src_ref=src, dst_ref=dst, send_sem=send, recv_sem=recv, device_id=who, device_id_type=MESH
        )

    acts = pl.ds(0, wide_a)
    grads = pl.ds(wide_a, wide_g)

    def q_rows(whose, m):
        return pl.ds(pl.multiple_of(whose * half + m * chunk, chunk), chunk)

    def m_rows(m):
        return pl.ds(m * chunk, chunk)

    def hop1(m, to_core, j):
        src, cols = ((qa_hbm, acts), (qg_hbm, grads))[j]
        to_core_id = core if to_core == 0 else other
        return remote(
            src.at[q_rows(to_core_id, m), :],
            qbuf.at[1, core, m_rows(m), cols],
            z1_send.at[m, to_core, j],
            z1_recv.at[m, to_core, j],
            (up, plane + to_core_id),
        )

    def hop1_arrival(m, from_core, j):
        src, cols = ((qa_hbm, acts), (qg_hbm, grads))[j]
        from_core_id = core if from_core == 0 else other
        return remote(
            src.at[q_rows(core, m), :],
            qbuf.at[1, from_core_id, m_rows(m), cols],
            z1_send.at[m, from_core, j],
            z1_recv.at[m, from_core, j],
            (up, plane + from_core_id),
        )

    def hop2(m):
        return remote(
            qbuf.at[1, :, m_rows(m), :],
            qbuf.at[2, :, m_rows(m), :],
            z2_send.at[m],
            z2_recv.at[m],
            (up, place),
        )

    def t_rows(p):
        return pl.ds(p * part, part)

    def t_down(p, j):
        src, cols = ((ta_hbm, acts), (tg_hbm, grads))[j]
        return remote(
            src.at[t_rows(p), :],
            tbuf.at[1, core, t_rows(p), cols],
            tz_send.at[p, j],
            tz_recv.at[p, j],
            (down, place),
        )

    def t_forward(p, whose):
        return remote(
            tbuf.at[1, whose, t_rows(p), :],
            tbuf.at[1, whose, t_rows(p), :],
            tf_send.at[p],
            tf_recv.at[p],
            sibling,
        )

    def swap(j, whose_q, whose):
        src, dst = (
            (qa_hbm.at[pl.ds(pl.multiple_of(whose_q * half, half), half), :], qbuf.at[0, whose, :, acts]),
            (qg_hbm.at[pl.ds(pl.multiple_of(whose_q * half, half), half), :], qbuf.at[0, whose, :, grads]),
            (ta_hbm, tbuf.at[0, whose, :, acts]),
            (tg_hbm, tbuf.at[0, whose, :, grads]),
        )[j]
        return src, dst

    def swap_out(j):
        src, dst = swap(j, other, core)
        return remote(src, dst, own_send.at[j], own_recv.at[j], sibling)

    def swap_in(j):
        src, dst = swap(j, core, other)
        return remote(src, dst, own_send.at[j], own_recv.at[j], sibling)

    def local(j):
        src, dst = swap(j, core, core)
        return pltpu.make_async_copy(src, dst, local_sem.at[j])

    seg_copy = remote(tseg_ref, segn, f_send.at[0], f_recv.at[0], (down, place))

    for j in range(4):
        local(j).start()
    for to_core in range(2):
        for j in range(2):
            hop1(0, to_core, j).start()
    for j in range(4):
        swap_out(j).start()
    for j in range(2):
        t_down(0, j).start()
    for m in range(1, CHUNKS):
        for to_core in range(2):
            for j in range(2):
                hop1(m, to_core, j).start()
    for p in range(1, TPARTS):
        for j in range(2):
            t_down(p, j).start()
    seg_copy.start()

    def compute(r, m):
        t_slot = 1 if r == 3 else 0
        q_slot = min(r, 2)
        tile = 256

        def body(n, carry):
            at = pl.ds(pl.multiple_of(n * tile, tile), tile)
            for which, cols in ((0, acts), (1, grads)):
                total = None
                for h in range(NCORE):
                    term = lax.dot_general(
                        qbuf[q_slot, h, m_rows(m), cols],
                        tbuf[t_slot, h, at, cols],
                        CONTRACT,
                        preferred_element_type=jnp.float32,
                    )
                    total = term if total is None else total + term
                gram[r, m, :, which, :, at] = total.reshape(NY, ry, tile)
            return carry

        lax.fori_loop(0, rows_t // tile, body, 0)

    def y_copy(r, m, d):
        return remote(
            gram.at[r, m, y_of(d)],
            yrecv.at[r, m, d - 1],
            y_send.at[r, m, d - 1],
            y_recv.at[r, m, d - 1],
            y_peer(d),
        )

    def x_copy(r, m):
        return remote(
            xsend.at[r, m, 1 - my_x], xrecv.at[r, m], x_send.at[r, m], x_recv.at[r, m], x_peer
        )

    def y_finish(r, m):
        for d in range(1, NY):
            y_copy(r, m, d).wait_recv()
        total = gram[r, m, my_y] + yrecv[r, m, 0] + yrecv[r, m, 1] + yrecv[r, m, 2]
        for x in range(NX):
            xsend[r, m, x] = total[:, :, x * lx : (x + 1) * lx]
        x_copy(r, m).start()

    def x_finish(r, m):
        x_copy(r, m).wait_recv()
        act = xsend[r, m, my_x, 0] + xrecv[r, m, 0]
        grad = xsend[r, m, my_x, 1] + xrecv[r, m, 1]
        pairs[r, pl.ds(m * ry, ry), :] = act * grad

    def segment_sum(r):
        seg_t = (segn if r == 3 else tseg_ref)[:, pl.ds(pl.multiple_of(my_x * lx, lx), lx)]
        onehot_t = (lax.broadcasted_iota(jnp.int32, (ST, lx), 0) == seg_t).astype(jnp.float32)
        q_slot = min(r, 2)
        owner = lax.rem(doc + n_doc - q_slot, n_doc)
        seg_q = qseg_ref[pl.ds(owner, 1), :]
        row = lax.broadcasted_iota(jnp.int32, (CHUNKS * ry, rows_q), 0)
        token = lax.broadcasted_iota(jnp.int32, (CHUNKS * ry, rows_q), 1)
        mine = core * half + (row // ry) * chunk + my_y * ry + row % ry
        ids = jnp.sum(jnp.where(token == mine, seg_q, 0), axis=1, keepdims=True)
        lane = lax.broadcasted_iota(jnp.int32, (CHUNKS * ry, LANES), 1)
        onehot_q = (lane == ids + r * SQ).astype(jnp.float32)
        left = lax.dot_general(
            onehot_t,
            pairs[r],
            CONTRACT,
            precision=lax.Precision.HIGHEST,
            preferred_element_type=jnp.float32,
        )
        return jnp.dot(
            left, onehot_q, precision=lax.Precision.HIGHEST, preferred_element_type=jnp.float32
        )

    todo_y, todo_x = [], []

    def finish(lag_y, lag_x):
        while len(todo_x) > lag_x:
            x_finish(*todo_x.pop(0))
        while len(todo_y) > lag_y:
            unit = todo_y.pop(0)
            y_finish(*unit)
            todo_x.append(unit)

    def unit(r, m):
        compute(r, m)
        for d in range(1, NY):
            y_copy(r, m, d).start()
        todo_y.append((r, m))

    def forward(p):
        for j in range(2):
            t_down(p, j).wait_recv()
        t_forward(p, core).start()

    for j in range(4):
        local(j).wait()
        swap_in(j).wait_recv()
    for m in range(CHUNKS):
        unit(0, m)
        finish(1, 1)
    for m in range(CHUNKS):
        for from_core in range(2):
            for j in range(2):
                hop1_arrival(m, from_core, j).wait_recv()
        hop2(m).start()
        unit(1, m)
        if m == 1:
            forward(0)
        if m == 3:
            forward(1)
        finish(1, 1)
    for m in range(2):
        hop2(m).wait_recv()
        unit(2, m)
        forward(2 + m)
        finish(1, 1)
    for p in range(TPARTS):
        t_forward(p, other).wait_recv()
    for m in range(2):
        unit(3, m)
        finish(1, 1)
    for m in range(2, CHUNKS):
        hop2(m).wait_recv()
        unit(3, m)
        finish(1, 1)
        unit(2, m)
        finish(1, 1)
    seg_copy.wait_recv()
    base = segment_sum(0) + segment_sum(1)
    finish(0, 1)
    finish(0, 1)

    fin[0] = segment_sum(3)
    third = remote(fin.at[0], fin.at[1], f_send.at[1], f_recv.at[1], (up, place))
    third.start()
    finish(0, 0)
    base = base + segment_sum(2)
    third.wait_recv()
    fin[2 + my_y] = base + fin[1]
    y_all = [
        remote(fin.at[2 + my_y], fin.at[2 + my_y], f_send.at[1 + d], f_recv.at[1 + d], y_peer(d))
        for d in range(1, NY)
    ]
    y_in = [
        remote(
            fin.at[2 + y_of(NY - d)],
            fin.at[2 + y_of(NY - d)],
            f_send.at[1 + d],
            f_recv.at[1 + d],
            y_peer(d),
        )
        for d in range(1, NY)
    ]
    for copy in y_all:
        copy.start()
    for copy in y_in:
        copy.wait_recv()
    fin[6] = (fin[2] + fin[3]) + (fin[4] + fin[5])
    x_all = remote(fin.at[6], fin.at[7], f_send.at[5], f_recv.at[5], x_peer)
    x_all.start()
    x_all.wait_recv()
    fin[8] = fin[6] + fin[7]
    core_all = remote(fin.at[8], fin.at[9], f_send.at[6], f_recv.at[6], sibling)
    core_all.start()
    core_all.wait_recv()
    out_ref[...] = ((fin[8] + fin[9]) * factor)[:, : CYCLE * SQ]

    seg_copy.wait_send()
    third.wait_send()
    for copy in y_all:
        copy.wait_send()
    x_all.wait_send()
    core_all.wait_send()
    for j in range(4):
        swap_out(j).wait_send()
    for m in range(CHUNKS):
        for to_core in range(2):
            for j in range(2):
                hop1(m, to_core, j).wait_send()
        hop2(m).wait_send()
    for p in range(TPARTS):
        for j in range(2):
            t_down(p, j).wait_send()
        t_forward(p, core).wait_send()
    for r in range(CYCLE):
        for m in range(CHUNKS):
            for d in range(1, NY):
                y_copy(r, m, d).wait_send()
            x_copy(r, m).wait_send()


def on_device(n_doc, train_acts, train_grads, query_acts, query_grads, train_seg, query_seg):
    rows_t, wide_a = train_acts.shape
    rows_q, wide_g = query_grads.shape
    half = rows_q // NCORE
    chunk = half // CHUNKS
    ry = chunk // NY
    lx = rows_t // NX
    wide = wide_a + wide_g
    dma = pltpu.SemaphoreType.DMA
    anywhere = pl.BlockSpec(memory_space=pl.ANY)
    vmem = pl.BlockSpec(memory_space=pltpu.VMEM)
    return pl.pallas_call(
        functools.partial(kernel, n_doc),
        out_shape=jax.ShapeDtypeStruct((ST, CYCLE * SQ), jnp.float32),
        in_specs=[anywhere] * 4 + [vmem] * 2,
        out_specs=vmem,
        scratch_shapes=[
            pltpu.VMEM((2, NCORE, rows_t, wide), jnp.bfloat16),
            pltpu.VMEM((3, NCORE, half, wide), jnp.bfloat16),
            pltpu.VMEM((CYCLE, CHUNKS, NY, 2, ry, rows_t), jnp.float32),
            pltpu.VMEM((CYCLE, CHUNKS, NY - 1, 2, ry, rows_t), jnp.float32),
            pltpu.VMEM((CYCLE, CHUNKS, NX, 2, ry, lx), jnp.float32),
            pltpu.VMEM((CYCLE, CHUNKS, 2, ry, lx), jnp.float32),
            pltpu.VMEM((CYCLE, CHUNKS * ry, lx), jnp.float32),
            pltpu.VMEM((1, rows_t), jnp.int32),
            pltpu.VMEM((10, ST, LANES), jnp.float32),
            dma((4,)),
            dma((4,)),
            dma((4,)),
            dma((CHUNKS, 2, 2)),
            dma((CHUNKS, 2, 2)),
            dma((CHUNKS,)),
            dma((CHUNKS,)),
            dma((TPARTS, 2)),
            dma((TPARTS, 2)),
            dma((TPARTS,)),
            dma((TPARTS,)),
            dma((CYCLE, CHUNKS, NY - 1)),
            dma((CYCLE, CHUNKS, NY - 1)),
            dma((CYCLE, CHUNKS)),
            dma((CYCLE, CHUNKS)),
            dma((7,)),
            dma((7,)),
        ],
        compiler_params=pltpu.CompilerParams(
            collective_id=0, has_side_effects=True, vmem_limit_bytes=56 * 1024 * 1024
        ),
        name="influence",
    )(train_acts, train_grads, query_acts, query_grads, train_seg, query_seg)


def solution(mesh):
    in_specs = (
        P("doc", "hidden"),
        P("doc", "hidden"),
        P("doc", "hidden"),
        P("doc", "hidden"),
        P("doc", None),
        P(),
    )
    return jax.shard_map(
        functools.partial(on_device, mesh.shape["doc"]),
        mesh=mesh,
        in_specs=in_specs,
        out_specs=P("doc", None),
        check_vma=False,
    )
```

time: 502 us -> 188 us (0.37)
  waiting for transfers between devices: 383 us -> 0 us
  Pallas kernels: 0 us -> 187 us
  blocking collectives: 53.1 us -> 0 us
  local copies, waits for them, and re-layouts: 24.3 us -> 1.28 us
  between operations: 13.4 us -> 0.01 us
  matrix products: 12.5 us -> 0 us
  other arithmetic: 8.18 us -> 0 us
    unnamed x8 -> x0, waiting for transfers between devices: 218 us -> none
    pallas_call x0 -> x1, Pallas kernels: none -> 187 us  [on_device(): pl.pallas_call(functools.partial(kernel, n_doc), out_shape=jax.ShapeDtype...]
    ppermute x6 -> x0, waiting for transfers between devices: 165 us -> none  [from_behind(): lax.ppermute(value, axis, [(i, (i + by) % devices) for i in range(devices)])]
    psum x1 -> x0, blocking collectives: 53.1 us -> none  [on_device(): totals = [lax.psum(part, 'hidden') for part in partials]]
    unnamed x26 -> x1, local copies, waits for them, and re-layouts: 18.9 us -> 1.28 us
    dot_general x16 -> x0, matrix products: 12.5 us -> none  [the longest x4 6.48 us: tally(): lax.dot_general(train_acts, cols_a, contract, preferred_element_type=jnp....]
    concatenate x5 -> x0, other arithmetic: 8.18 us -> none  [the longest x4 7.51 us: tally(): jnp.concatenate([act_gram, grad_gram], axis=1)]
  transfers between devices with their start and end apart: 10 -> 0, of which waited for: 7 -> 0; matrix products, arithmetic and copies ran while one was open for 6% -> 0% of each run, Pallas kernels for 0% -> 0%
where the time goes in v1:
time: 188 us
  Pallas kernels  187 us (99%)
    pallas_call x1, Pallas kernels, on_device(): pl.pallas_call(functools.partial(kernel, n_doc), out_shape=jax.ShapeDtype...  187 us

profile of v1, /device:TPU:1, one launch (start us, length us, event | category | flops | bytes accessed | tf_op | source)
XLA Modules:
  0.0 188.2 jit_solution(15640124823808481006)
XLA Ops:
  0.0 186.9 %influence.1 = f32[8,32]{1,0:T(8,128)} custom-call(bf16[768,1792]{1,0:T(8,128)(2,1)} %ta_hbm.1, bf16[768,512]{1,0:T(8,128)(2,1)} %tg_hbm.1, bf16[512,1792]{1,0:T(8,128)(2,1)} %qa_hbm.1, bf16[512,512]{1,0:T(8,128)(2,1)} %qg_hbm.1, s32[1,768]{1,0:T(1,128)} %tseg_ref.1, s32[16,512]{1,0:T(8,128)} %qseg_ref.1), custom_call_target="tpu_custom_call" | custom-call | tf_op jit(solution)/shard_map/influence/pallas_call | solution.py:404
  186.9 1.3 copy.8

commit v2 on v0

v2 whole, which is shorter than its diff:
```python
import functools
import math

import jax
import jax.numpy as jnp
from jax import lax
from jax.experimental import pallas as pl
from jax.experimental.pallas import tpu as pltpu
from jax.sharding import PartitionSpec as P

ST = 8
SQ = 8
CYCLE = 4
NY = 4
NX = 2
NCORE = 2
CHUNKS = 4
TPARTS = 3
LANES = 128
ACT = 0
GRAD = 1
MESH = pl.DeviceIdType.MESH
CONTRACT = (((1,), (1,)), ((), ()))
F32 = jnp.float32

UNITS = {
    "g0": (GRAD, 0, 0, 4, 0, 3),
    "a0": (ACT, 0, 0, 4, 0, 3),
    "g1": (GRAD, 1, 0, 4, 0, 3),
    "g2": (GRAD, 2, 0, 4, 0, 3),
    "g3": (GRAD, 3, 0, 4, 0, 3),
    "a1_01": (ACT, 1, 0, 2, 0, 3),
    "a1_23": (ACT, 1, 2, 2, 0, 3),
    "a2_0": (ACT, 2, 0, 1, 0, 3),
    "a2_1": (ACT, 2, 1, 1, 0, 3),
    "a2_2": (ACT, 2, 2, 1, 0, 3),
    "a2_3": (ACT, 2, 3, 1, 0, 3),
    "a3_01": (ACT, 3, 0, 2, 0, 2),
    "a3_2": (ACT, 3, 2, 1, 0, 2),
    "a3_3": (ACT, 3, 3, 1, 0, 2),
    "a3_all": (ACT, 3, 0, 4, 2, 1),
}
ORDER = list(UNITS)


def kernel(
    n_doc,
    ta_hbm,
    tg_hbm,
    qa_hbm,
    qg_hbm,
    tseg_ref,
    qseg_ref,
    out_ref,
    ta,
    tg,
    qa,
    qg,
    gram,
    yin,
    xin,
    done,
    gin,
    segn,
    small,
    fin_y,
    fin_x,
    local_sem,
    own_send,
    own_recv,
    qg_send,
    qg_recv,
    qa_send,
    qa_recv,
    hop_send,
    hop_recv,
    tg_send,
    tg_recv,
    ta_send,
    ta_recv,
    tgf_send,
    tgf_recv,
    taf_send,
    taf_recv,
    y_send,
    y_recv,
    x_send,
    x_recv,
    g_send,
    g_recv,
    s_send,
    s_recv,
    fy_send,
    fy_recv,
    fx_send,
    fx_recv,
):
    rows_t, wide_a = ta_hbm.shape
    rows_q, wide_g = qg_hbm.shape
    half = rows_q // NCORE
    chunk = half // CHUNKS
    part = rows_t // TPARTS
    ry = chunk // (NY * NX)
    factor = math.sqrt(ST * SQ / (rows_t * rows_q))

    doc = lax.axis_index("doc")
    place = lax.axis_index("hidden")
    core = lax.rem(place, NCORE)
    other = 1 - core
    my_x = lax.rem(place // NCORE, NX)
    my_y = place // (NCORE * NX)
    up = lax.rem(doc + 1, n_doc)
    down = lax.rem(doc + n_doc - 1, n_doc)

    def y_of(d):
        return lax.rem(my_y + d, NY)

    def spot(y, x, c):
        return y * (NX * NCORE) + x * NCORE + c

    sibling = (doc, spot(my_y, my_x, other))
    x_peer = (doc, spot(my_y, 1 - my_x, core))
    x_other = (doc, spot(my_y, 1 - my_x, other))

    def y_peer(d, of=doc):
        return (of, spot(y_of(d), my_x, core))

    greet = [sibling, x_peer, x_other]
    greet += [(up, spot(my_y, my_x, other)), (down, spot(my_y, my_x, other))]
    greet += [y_peer(d) for d in range(1, NY)]
    greet += [y_peer(d, up) for d in range(NY)]
    greet += [y_peer(d, down) for d in range(NY)]
    barrier = pltpu.get_barrier_semaphore()
    for who in greet:
        pl.semaphore_signal(barrier, inc=1, device_id=who, device_id_type=MESH)
    pl.semaphore_wait(barrier, len(greet))

    def remote(src, dst, send, recv, who):
        return pltpu.make_async_remote_copy(
            src_ref=src, dst_ref=dst, send_sem=send, recv_sem=recv, device_id=who, device_id_type=MESH
        )

    def cols(wide, whose):
        return pl.ds(pl.multiple_of(whose * wide, LANES), wide)

    def q_half(whose):
        return pl.ds(pl.multiple_of(whose * half, half), half)

    def swap(j, whose_q, whose):
        return (
            (qg_hbm.at[q_half(whose_q), :], qg.at[0, :, cols(wide_g, whose)]),
            (tg_hbm, tg.at[0, :, cols(wide_g, whose)]),
            (qa_hbm.at[q_half(whose_q), :], qa.at[0, :, cols(wide_a, whose)]),
            (ta_hbm, ta.at[0, :, cols(wide_a, whose)]),
        )[j]

    def swap_out(j):
        return remote(*swap(j, other, core), own_send.at[j], own_recv.at[j], sibling)

    def swap_in(j):
        return remote(*swap(j, core, other), own_send.at[j], own_recv.at[j], sibling)

    def local(j):
        return pltpu.make_async_copy(*swap(j, core, core), local_sem.at[j])

    def who_up(far):
        return core if far == 0 else other

    def qg_up(far):
        to = who_up(far)
        return remote(
            qg_hbm.at[q_half(to), :],
            qg.at[1, :, cols(wide_g, core)],
            qg_send.at[far],
            qg_recv.at[far],
            (up, spot(my_y, my_x, to)),
        )

    def qg_arrival(far):
        return remote(
            qg_hbm.at[q_half(core), :],
            qg.at[1, :, cols(wide_g, who_up(far))],
            qg_send.at[far],
            qg_recv.at[far],
            (up, spot(my_y, my_x, who_up(far))),
        )

    def q_chunk(m):
        return pl.ds(m * chunk, chunk)

    def qa_up(m, far):
        to = who_up(far)
        return remote(
            qa_hbm.at[pl.ds(pl.multiple_of(to * half + m * chunk, chunk), chunk), :],
            qa.at[1, q_chunk(m), cols(wide_a, core)],
            qa_send.at[m, far],
            qa_recv.at[m, far],
            (up, spot(my_y, my_x, to)),
        )

    def qa_arrival(m, far):
        return remote(
            qa_hbm.at[pl.ds(pl.multiple_of(core * half + m * chunk, chunk), chunk), :],
            qa.at[1, q_chunk(m), cols(wide_a, who_up(far))],
            qa_send.at[m, far],
            qa_recv.at[m, far],
            (up, spot(my_y, my_x, who_up(far))),
        )

    def qa_hop(m):
        return remote(
            qa.at[1, q_chunk(m), :], qa.at[2, q_chunk(m), :], hop_send.at[m], hop_recv.at[m], (up, place)
        )

    def tg_down(step):
        src = tg_hbm if step == 0 else tg.at[step, :, cols(wide_g, core)]
        return remote(
            src, tg.at[step + 1, :, cols(wide_g, core)], tg_send.at[step], tg_recv.at[step], (down, place)
        )

    def tg_across(step, whose):
        ref = tg.at[step + 1, :, cols(wide_g, whose)]
        return remote(ref, ref, tgf_send.at[step], tgf_recv.at[step], sibling)

    def t_part(p):
        return pl.ds(p * part, part)

    def ta_down(p):
        return remote(
            ta_hbm.at[t_part(p), :],
            ta.at[1, t_part(p), cols(wide_a, core)],
            ta_send.at[p],
            ta_recv.at[p],
            (down, place),
        )

    def ta_across(p, whose):
        ref = ta.at[1, t_part(p), cols(wide_a, whose)]
        return remote(ref, ref, taf_send.at[p], taf_recv.at[p], sibling)

    seg_copy = remote(tseg_ref, segn, s_send, s_recv, (down, place))

    def area(name):
        kind, r, m, n, p, k = UNITS[name]
        return kind, r, pl.ds(m * ry, n * ry), pl.ds(p * part, k * part)

    def compute(name):
        kind, r, m, n, p, k = UNITS[name]
        if kind == ACT:
            query, train = qa.at[min(r, 2)], ta.at[1 if r == 3 else 0]
        else:
            query, train = qg.at[min(r, 1)], tg.at[max(r - 1, 0)]
        left = query[m * chunk : (m + n) * chunk, :]
        right = train[p * part : (p + k) * part, :]
        if n == CHUNKS:
            total = lax.dot_general(left, right, CONTRACT, preferred_element_type=F32)
        else:
            total = lax.dot_general(right, left, CONTRACT, preferred_element_type=F32).T
        for i in range(n):
            gram[kind, r, :, :, (m + i) * ry : (m + i + 1) * ry, p * part : (p + k) * part] = total[
                i * chunk : (i + 1) * chunk
            ].reshape(NY, NX, ry, k * part)

    def y_copy(name, d):
        kind, r, rows, lanes = area(name)
        u = ORDER.index(name)
        return remote(
            gram.at[kind, r, y_of(d), :, rows, lanes],
            yin.at[kind, r, d - 1, :, rows, lanes],
            y_send.at[u, d - 1],
            y_recv.at[u, d - 1],
            y_peer(d),
        )

    def x_copy(name):
        kind, r, rows, lanes = area(name)
        u = ORDER.index(name)
        return remote(
            gram.at[kind, r, my_y, 1 - my_x, rows, lanes],
            xin.at[kind, r, rows, lanes],
            x_send.at[u],
            x_recv.at[u],
            x_peer,
        )

    def g_move(r):
        return remote(done.at[GRAD, r], gin.at[r - 2], g_send.at[r - 2], g_recv.at[r - 2], (up, place))

    def unit(name):
        compute(name)
        for d in range(1, NY):
            y_copy(name, d).start()

    def y_finish(name):
        kind, r, rows, lanes = area(name)
        for d in range(1, NY):
            y_copy(name, d).wait_recv()
        gram[kind, r, my_y, :, rows, lanes] = (
            gram[kind, r, my_y, :, rows, lanes] + yin[kind, r, 0, :, rows, lanes]
        ) + (yin[kind, r, 1, :, rows, lanes] + yin[kind, r, 2, :, rows, lanes])
        x_copy(name).start()

    def x_finish(name):
        kind, r, rows, lanes = area(name)
        x_copy(name).wait_recv()
        done[kind, r, rows, lanes] = gram[kind, r, my_y, my_x, rows, lanes] + xin[kind, r, rows, lanes]

    def onehots(r):
        seg_t = (segn if r == 3 else tseg_ref)[...]
        onehot_t = (lax.broadcasted_iota(jnp.int32, (ST, rows_t), 0) == seg_t).astype(F32)
        owner = lax.rem(doc + n_doc - min(r, 2), n_doc)
        seg_q = qseg_ref[pl.ds(owner, 1), :]
        row = lax.broadcasted_iota(jnp.int32, (CHUNKS * ry, rows_q), 0)
        token = lax.broadcasted_iota(jnp.int32, (CHUNKS * ry, rows_q), 1)
        mine = core * half + (row // ry) * chunk + my_y * (NX * ry) + my_x * ry + row % ry
        ids = jnp.sum(jnp.where(token == mine, seg_q, 0), axis=1, keepdims=True)
        lane = lax.broadcasted_iota(jnp.int32, (CHUNKS * ry, LANES), 1)
        return onehot_t, (lane == ids + r * SQ).astype(F32)

    def segment_sum(r, hots):
        onehot_t, onehot_q = hots
        grads = gin[r - 2] if r >= 2 else done[GRAD, r]
        left = lax.dot_general(
            onehot_t,
            done[ACT, r] * grads,
            CONTRACT,
            precision=lax.Precision.HIGHEST,
            preferred_element_type=F32,
        )
        return jnp.dot(left, onehot_q, precision=lax.Precision.HIGHEST, preferred_element_type=F32)

    def arrive_and_hop(m):
        for far in range(2):
            qa_arrival(m, far).wait_recv()
        qa_hop(m).start()

    for far in range(2):
        qg_up(far).start()
    tg_down(0).start()
    for j in range(4):
        swap_out(j).start()
        local(j).start()
    for far in range(2):
        qa_up(0, far).start()
    ta_down(0).start()
    for m in range(1, CHUNKS):
        for far in range(2):
            qa_up(m, far).start()
    seg_copy.start()

    for j in range(2):
        local(j).wait()
        swap_in(j).wait_recv()
    unit("g0")
    for j in range(2, 4):
        local(j).wait()
        swap_in(j).wait_recv()
    unit("a0")
    for far in range(2):
        qg_arrival(far).wait_recv()
    unit("g1")
    tg_down(0).wait_recv()
    tg_down(1).start()
    tg_across(0, core).start()
    for p in range(1, TPARTS):
        ta_down(p).start()
    tg_across(0, other).wait_recv()
    unit("g2")
    arrive_and_hop(0)
    y_finish("g0")
    y_finish("a0")
    arrive_and_hop(1)
    unit("a1_01")
    x_finish("g0")
    x_finish("a0")
    ta_down(0).wait_recv()
    ta_across(0, core).start()
    y_finish("g1")
    arrive_and_hop(2)
    y_finish("g2")
    x_finish("g1")
    arrive_and_hop(3)
    unit("a1_23")
    x_finish("g2")
    g_move(2).start()
    y_finish("a1_01")
    tg_down(1).wait_recv()
    tg_across(1, core).start()
    tg_across(1, other).wait_recv()
    unit("g3")
    x_finish("a1_01")
    qa_hop(0).wait_recv()
    unit("a2_0")
    y_finish("a1_23")
    y_finish("g3")
    qa_hop(1).wait_recv()
    unit("a2_1")
    x_finish("a1_23")
    x_finish("g3")
    g_move(3).start()
    y_finish("a2_0")
    ta_down(1).wait_recv()
    ta_across(1, core).start()
    base = segment_sum(0, onehots(0)) + segment_sum(1, onehots(1))
    seg_copy.wait_recv()
    hots_2, hots_3 = onehots(2), onehots(3)
    for p in range(2):
        ta_across(p, other).wait_recv()
    unit("a3_01")
    x_finish("a2_0")
    y_finish("a2_1")
    qa_hop(2).wait_recv()
    unit("a2_2")
    unit("a3_2")
    y_finish("a3_01")
    x_finish("a2_1")
    y_finish("a2_2")
    y_finish("a3_2")
    x_finish("a3_01")
    ta_down(2).wait_recv()
    ta_across(2, core).start()
    qa_hop(3).wait_recv()
    unit("a3_3")
    unit("a2_3")
    ta_across(2, other).wait_recv()
    unit("a3_all")
    x_finish("a2_2")
    x_finish("a3_2")
    y_finish("a3_3")
    y_finish("a2_3")
    y_finish("a3_all")
    for r in range(2, CYCLE):
        g_move(r).wait_recv()
    x_finish("a2_3")
    fin_y[0, my_y] = base + segment_sum(2, hots_2)
    fy = [
        remote(fin_y.at[0, my_y], fin_y.at[0, my_y], fy_send.at[0, d], fy_recv.at[0, my_y], y_peer(d))
        for d in range(1, NY)
    ]
    for copy in fy:
        copy.start()
    x_finish("a3_3")
    x_finish("a3_all")
    small[...] = segment_sum(3, hots_3)
    fu = [
        remote(small, fin_y.at[1, my_y], fy_send.at[1, d], fy_recv.at[1, my_y], y_peer(d, up))
        for d in range(NY)
    ]
    for copy in fu:
        copy.start()
    for d in range(1, NY):
        y = y_of(d)
        remote(fin_y.at[0, y], fin_y.at[0, y], fy_send.at[0, d], fy_recv.at[0, y], y_peer(d)).wait_recv()
    for d in range(NY):
        y = y_of(d)
        remote(small, fin_y.at[1, y], fy_send.at[1, d], fy_recv.at[1, y], y_peer(d, up)).wait_recv()
    total = fin_y[0, 0] + fin_y[1, 0]
    for y in range(1, NY):
        total = total + (fin_y[0, y] + fin_y[1, y])
    mine = lax.rem(place, NX * NCORE)
    fin_x[mine] = total
    fx = []
    for i, who in enumerate((sibling, x_peer, x_other)):
        fx.append(remote(fin_x.at[mine], fin_x.at[mine], fx_send.at[i], fx_recv.at[mine], who))
        fx[-1].start()
    for i, (x, c) in enumerate(((my_x, other), (1 - my_x, core), (1 - my_x, other))):
        at = x * NCORE + c
        remote(fin_x.at[at], fin_x.at[at], fx_send.at[i], fx_recv.at[at], sibling).wait_recv()
    out_ref[...] = (((fin_x[0] + fin_x[1]) + (fin_x[2] + fin_x[3])) * factor)[:, : CYCLE * SQ]

    seg_copy.wait_send()
    for copy in fy + fu + fx:
        copy.wait_send()
    for j in range(4):
        swap_out(j).wait_send()
    for far in range(2):
        qg_up(far).wait_send()
    for m in range(CHUNKS):
        for far in range(2):
            qa_up(m, far).wait_send()
        qa_hop(m).wait_send()
    for step in range(2):
        tg_down(step).wait_send()
        tg_across(step, core).wait_send()
    for p in range(TPARTS):
        ta_down(p).wait_send()
        ta_across(p, core).wait_send()
    for r in range(2, CYCLE):
        g_move(r).wait_send()
    for name in ORDER:
        for d in range(1, NY):
            y_copy(name, d).wait_send()
        x_copy(name).wait_send()


def on_device(n_doc, train_acts, train_grads, query_acts, query_grads, train_seg, query_seg):
    rows_t, wide_a = train_acts.shape
    rows_q, wide_g = query_grads.shape
    half = rows_q // NCORE
    rows = half // (NY * NX)
    units = len(ORDER)
    dma = pltpu.SemaphoreType.DMA
    anywhere = pl.BlockSpec(memory_space=pl.ANY)
    vmem = pl.BlockSpec(memory_space=pltpu.VMEM)
    bf16 = jnp.bfloat16

    def pair(*shape):
        return [dma(shape), dma(shape)]

    return pl.pallas_call(
        functools.partial(kernel, n_doc),
        out_shape=jax.ShapeDtypeStruct((ST, CYCLE * SQ), F32),
        in_specs=[anywhere] * 4 + [vmem] * 2,
        out_specs=vmem,
        scratch_shapes=[
            pltpu.VMEM((2, rows_t, NCORE * wide_a), bf16),
            pltpu.VMEM((3, rows_t, NCORE * wide_g), bf16),
            pltpu.VMEM((3, half, NCORE * wide_a), bf16),
            pltpu.VMEM((2, half, NCORE * wide_g), bf16),
            pltpu.VMEM((2, CYCLE, NY, NX, rows, rows_t), F32),
            pltpu.VMEM((2, CYCLE, NY - 1, NX, rows, rows_t), F32),
            pltpu.VMEM((2, CYCLE, rows, rows_t), F32),
            pltpu.VMEM((2, CYCLE, rows, rows_t), F32),
            pltpu.VMEM((2, rows, rows_t), F32),
            pltpu.VMEM((1, rows_t), jnp.int32),
            pltpu.VMEM((ST, LANES), F32),
            pltpu.VMEM((2, NY, ST, LANES), F32),
            pltpu.VMEM((NX * NCORE, ST, LANES), F32),
            dma((4,)),
            *pair(4),
            *pair(2),
            *pair(CHUNKS, 2),
            *pair(CHUNKS),
            *pair(2),
            *pair(TPARTS),
            *pair(2),
            *pair(TPARTS),
            *pair(units, NY - 1),
            *pair(units),
            *pair(2),
            dma,
            dma,
            *pair(2, NY),
            *pair(NX * NCORE),
        ],
        compiler_params=pltpu.CompilerParams(
            collective_id=0, has_side_effects=True, vmem_limit_bytes=56 * 1024 * 1024
        ),
        name="influence",
    )(train_acts, train_grads, query_acts, query_grads, train_seg, query_seg)


def solution(mesh):
    in_specs = (
        P("doc", "hidden"),
        P("doc", "hidden"),
        P("doc", "hidden"),
        P("doc", "hidden"),
        P("doc", None),
        P(),
    )
    return jax.shard_map(
        functools.partial(on_device, mesh.shape["doc"]),
        mesh=mesh,
        in_specs=in_specs,
        out_specs=P("doc", None),
        check_vma=False,
    )
```

time: 502 us -> 179 us (0.36)
  waiting for transfers between devices: 383 us -> 0 us
  Pallas kernels: 0 us -> 177 us
  blocking collectives: 53.1 us -> 0 us
  local copies, waits for them, and re-layouts: 24.3 us -> 1.28 us
  between operations: 13.4 us -> 0.01 us
  matrix products: 12.5 us -> 0 us
  other arithmetic: 8.18 us -> 0 us
    unnamed x8 -> x0, waiting for transfers between devices: 218 us -> none
    pallas_call x0 -> x1, Pallas kernels: none -> 177 us  [on_device(): pl.pallas_call(functools.partial(kernel, n_doc), out_shape=jax.ShapeDtype...]
    ppermute x6 -> x0, waiting for transfers between devices: 165 us -> none  [from_behind(): lax.ppermute(value, axis, [(i, (i + by) % devices) for i in range(devices)])]
    psum x1 -> x0, blocking collectives: 53.1 us -> none  [on_device(): totals = [lax.psum(part, 'hidden') for part in partials]]
    unnamed x26 -> x1, local copies, waits for them, and re-layouts: 18.9 us -> 1.28 us
    dot_general x16 -> x0, matrix products: 12.5 us -> none  [the longest x4 6.48 us: tally(): lax.dot_general(train_acts, cols_a, contract, preferred_element_type=jnp....]
    concatenate x5 -> x0, other arithmetic: 8.18 us -> none  [the longest x4 7.51 us: tally(): jnp.concatenate([act_gram, grad_gram], axis=1)]
  transfers between devices with their start and end apart: 10 -> 0, of which waited for: 7 -> 0; matrix products, arithmetic and copies ran while one was open for 6% -> 0% of each run, Pallas kernels for 0% -> 0%
where the time goes in v2:
time: 179 us; the launch traced here: 178 us
  Pallas kernels  177 us (99%)
    pallas_call x1, Pallas kernels, on_device(): pl.pallas_call(functools.partial(kernel, n_doc), out_shape=jax.ShapeDtype...  177 us

profile of v2, /device:TPU:1, one launch (start us, length us, event | category | flops | bytes accessed | tf_op | source)
XLA Modules:
  0.0 178.5 jit_solution(16139413725055105697)
XLA Ops:
  0.0 177.2 %influence.1 = f32[8,32]{1,0:T(8,128)} custom-call(bf16[768,1792]{1,0:T(8,128)(2,1)} %ta_hbm.1, bf16[768,512]{1,0:T(8,128)(2,1)} %tg_hbm.1, bf16[512,1792]{1,0:T(8,128)(2,1)} %qa_hbm.1, bf16[512,512]{1,0:T(8,128)(2,1)} %qg_hbm.1, s32[1,768]{1,0:T(1,128)} %tseg_ref.1, s32[16,512]{1,0:T(8,128)} %qseg_ref.1), custom_call_target="tpu_custom_call" | custom-call | tf_op jit(solution)/shard_map/influence/pallas_call | solution.py:510
  177.2 1.3 copy.8

commit v3 on v2

--- a/solution.py
+++ b/solution.py
@@ -371,52 +371,48 @@
     y_finish("a0")
     arrive_and_hop(1)
     unit("a1_01")
-    x_finish("g0")
-    x_finish("a0")
+    y_finish("g1")
+    arrive_and_hop(2)
     ta_down(0).wait_recv()
     ta_across(0, core).start()
-    y_finish("g1")
-    arrive_and_hop(2)
     y_finish("g2")
-    x_finish("g1")
     arrive_and_hop(3)
     unit("a1_23")
-    x_finish("g2")
-    g_move(2).start()
-    y_finish("a1_01")
     tg_down(1).wait_recv()
     tg_across(1, core).start()
+    y_finish("a1_01")
     tg_across(1, other).wait_recv()
     unit("g3")
-    x_finish("a1_01")
     qa_hop(0).wait_recv()
     unit("a2_0")
     y_finish("a1_23")
-    y_finish("g3")
     qa_hop(1).wait_recv()
     unit("a2_1")
-    x_finish("a1_23")
-    x_finish("g3")
-    g_move(3).start()
+    y_finish("g3")
+    for name in ("g0", "a0", "g1", "g2"):
+        x_finish(name)
+    g_move(2).start()
     y_finish("a2_0")
     ta_down(1).wait_recv()
     ta_across(1, core).start()
+    for p in range(2):
+        ta_across(p, other).wait_recv()
+    unit("a3_01")
+    y_finish("a2_1")
+    for name in ("a1_01", "a1_23", "g3"):
+        x_finish(name)
+    g_move(3).start()
     base = segment_sum(0, onehots(0)) + segment_sum(1, onehots(1))
     seg_copy.wait_recv()
     hots_2, hots_3 = onehots(2), onehots(3)
-    for p in range(2):
-        ta_across(p, other).wait_recv()
-    unit("a3_01")
-    x_finish("a2_0")
-    y_finish("a2_1")
     qa_hop(2).wait_recv()
     unit("a2_2")
     unit("a3_2")
     y_finish("a3_01")
-    x_finish("a2_1")
+    for name in ("a2_0", "a2_1"):
+        x_finish(name)
     y_finish("a2_2")
     y_finish("a3_2")
-    x_finish("a3_01")
     ta_down(2).wait_recv()
     ta_across(2, core).start()
     qa_hop(3).wait_recv()
@@ -424,8 +420,8 @@
     unit("a2_3")
     ta_across(2, other).wait_recv()
     unit("a3_all")
-    x_finish("a2_2")
-    x_finish("a3_2")
+    for name in ("a3_01", "a2_2", "a3_2"):
+        x_finish(name)
     y_finish("a3_3")
     y_finish("a2_3")
     y_finish("a3_all")

time: 179 us -> 158 us (0.88)
  Pallas kernels: 177 us -> 156 us
    pallas_call x1, Pallas kernels: 177 us -> 156 us  [on_device(): pl.pallas_call(functools.partial(kernel, n_doc), out_shape=jax.ShapeDtype...]
where the time goes in v3:
time: 158 us
  Pallas kernels  156 us (99%)
    pallas_call x1, Pallas kernels, on_device(): pl.pallas_call(functools.partial(kernel, n_doc), out_shape=jax.ShapeDtype...  156 us

profile of v3, /device:TPU:1, one launch (start us, length us, event | category | flops | bytes accessed | tf_op | source)
XLA Modules:
  0.0 157.7 jit_solution(6812276992128145533)
XLA Ops:
  0.0 156.5 %influence.1 = f32[8,32]{1,0:T(8,128)} custom-call(bf16[768,1792]{1,0:T(8,128)(2,1)} %ta_hbm.1, bf16[768,512]{1,0:T(8,128)(2,1)} %tg_hbm.1, bf16[512,1792]{1,0:T(8,128)(2,1)} %qa_hbm.1, bf16[512,512]{1,0:T(8,128)(2,1)} %qg_hbm.1, s32[1,768]{1,0:T(1,128)} %tseg_ref.1, s32[16,512]{1,0:T(8,128)} %qseg_ref.1), custom_call_target="tpu_custom_call" | custom-call | tf_op jit(solution)/shard_map/influence/pallas_call | solution.py:506
  156.5 1.3 copy.8

commit v4 on v3

--- a/solution.py
+++ b/solution.py
@@ -22,6 +22,9 @@
 MESH = pl.DeviceIdType.MESH
 CONTRACT = (((1,), (1,)), ((), ()))
 F32 = jnp.float32
+I32 = jnp.int32
+TOP = 32767.0
+LEAST = 1e-34
 
 UNITS = {
     "g0": (GRAD, 0, 0, 4, 0, 3),
@@ -43,6 +46,33 @@
 ORDER = list(UNITS)
 
 
+def spread(tile, rows, lanes):
+    wide = jnp.concatenate([tile] * (lanes // LANES), axis=1) if lanes > LANES else tile
+    return jnp.concatenate([wide] * (rows // 8), axis=0) if rows > 8 else wide
+
+
+def highest(value):
+    rows, lanes = value.shape
+    top = jnp.max(jnp.abs(value).reshape(rows // 8, 8, lanes), axis=0)
+    return functools.reduce(
+        jnp.maximum, [top[:, b * LANES : (b + 1) * LANES] for b in range(lanes // LANES)]
+    )
+
+
+def squeeze(high, low):
+    scale = jnp.maximum(jnp.maximum(highest(high), highest(low)), LEAST)
+    times = spread(TOP / scale, *high.shape)
+    packed = jnp.round(high * times).astype(I32) * 65536 + jnp.round(low * times).astype(I32)
+    return packed, scale * (1.0 / TOP)
+
+
+def unsqueeze(packed, step):
+    high = lax.shift_right_arithmetic(packed + 32768, jnp.full_like(packed, 16))
+    low = packed - high * 65536
+    step = spread(step, *packed.shape)
+    return high.astype(F32) * step, low.astype(F32) * step
+
+
 def kernel(
     n_doc,
     ta_hbm,
@@ -57,8 +87,14 @@
     qa,
     qg,
     gram,
+    yout,
+    yout_step,
     yin,
+    yin_step,
+    xout,
+    xout_step,
     xin,
+    xin_step,
     done,
     gin,
     segn,
@@ -125,16 +161,6 @@
     def y_peer(d, of=doc):
         return (of, spot(y_of(d), my_x, core))
 
-    greet = [sibling, x_peer, x_other]
-    greet += [(up, spot(my_y, my_x, other)), (down, spot(my_y, my_x, other))]
-    greet += [y_peer(d) for d in range(1, NY)]
-    greet += [y_peer(d, up) for d in range(NY)]
-    greet += [y_peer(d, down) for d in range(NY)]
-    barrier = pltpu.get_barrier_semaphore()
-    for who in greet:
-        pl.semaphore_signal(barrier, inc=1, device_id=who, device_id_type=MESH)
-    pl.semaphore_wait(barrier, len(greet))
-
     def remote(src, dst, send, recv, who):
         return pltpu.make_async_remote_copy(
             src_ref=src, dst_ref=dst, send_sem=send, recv_sem=recv, device_id=who, device_id_type=MESH
@@ -260,27 +286,44 @@
             gram[kind, r, :, :, (m + i) * ry : (m + i + 1) * ry, p * part : (p + k) * part] = total[
                 i * chunk : (i + 1) * chunk
             ].reshape(NY, NX, ry, k * part)
+        u = ORDER.index(name)
+        _, _, rows, lanes = area(name)
+
+        def code(y, carry):
+            packed, step = squeeze(gram[kind, r, y, 0, rows, lanes], gram[kind, r, y, 1, rows, lanes])
+            yout[kind, r, y, rows, lanes] = packed
+            yout_step[u, y] = step
+            return carry
+
+        lax.fori_loop(0, NY, code, 0)
 
     def y_copy(name, d):
         kind, r, rows, lanes = area(name)
         u = ORDER.index(name)
-        return remote(
-            gram.at[kind, r, y_of(d), :, rows, lanes],
-            yin.at[kind, r, d - 1, :, rows, lanes],
-            y_send.at[u, d - 1],
-            y_recv.at[u, d - 1],
-            y_peer(d),
+        return (
+            remote(
+                yout.at[kind, r, y_of(d), rows, lanes],
+                yin.at[kind, r, d - 1, rows, lanes],
+                y_send.at[u, d - 1, 0],
+                y_recv.at[u, d - 1, 0],
+                y_peer(d),
+            ),
+            remote(
+                yout_step.at[u, y_of(d)],
+                yin_step.at[u, d - 1],
+                y_send.at[u, d - 1, 1],
+                y_recv.at[u, d - 1, 1],
+                y_peer(d),
+            ),
         )
 
     def x_copy(name):
-        kind, r, rows, lanes = area(name)
+        _, _, _, n, _, k = UNITS[name]
         u = ORDER.index(name)
-        return remote(
-            gram.at[kind, r, my_y, 1 - my_x, rows, lanes],
-            xin.at[kind, r, rows, lanes],
-            x_send.at[u],
-            x_recv.at[u],
-            x_peer,
+        piece = (u, pl.ds(0, n * ry), pl.ds(0, k * part // 2))
+        return (
+            remote(xout.at[piece], xin.at[piece], x_send.at[u, 0], x_recv.at[u, 0], x_peer),
+            remote(xout_step.at[u], xin_step.at[u], x_send.at[u, 1], x_recv.at[u, 1], x_peer),
         )
 
     def g_move(r):
@@ -289,21 +332,39 @@
     def unit(name):
         compute(name)
         for d in range(1, NY):
-            y_copy(name, d).start()
+            for copy in y_copy(name, d):
+                copy.start()
 
     def y_finish(name):
-        kind, r, rows, lanes = area(name)
+        kind, r, m, n, p, k = UNITS[name]
+        _, _, rows, lanes = area(name)
+        u = ORDER.index(name)
+        high, low = gram[kind, r, my_y, 0, rows, lanes], gram[kind, r, my_y, 1, rows, lanes]
         for d in range(1, NY):
-            y_copy(name, d).wait_recv()
-        gram[kind, r, my_y, :, rows, lanes] = (
-            gram[kind, r, my_y, :, rows, lanes] + yin[kind, r, 0, :, rows, lanes]
-        ) + (yin[kind, r, 1, :, rows, lanes] + yin[kind, r, 2, :, rows, lanes])
-        x_copy(name).start()
+            for copy in y_copy(name, d):
+                copy.wait_recv()
+            more = unsqueeze(yin[kind, r, d - 1, rows, lanes], yin_step[u, d - 1])
+            high, low = high + more[0], low + more[1]
+        gram[kind, r, my_y, 0, rows, lanes] = high
+        gram[kind, r, my_y, 1, rows, lanes] = low
+        go = gram[kind, r, my_y, 1 - my_x, rows, lanes]
+        wide = k * part // 2
+        packed, step = squeeze(go[:, :wide], go[:, wide:])
+        xout[u, : n * ry, :wide] = packed
+        xout_step[u] = step
+        for copy in x_copy(name):
+            copy.start()
 
     def x_finish(name):
-        kind, r, rows, lanes = area(name)
-        x_copy(name).wait_recv()
-        done[kind, r, rows, lanes] = gram[kind, r, my_y, my_x, rows, lanes] + xin[kind, r, rows, lanes]
+        kind, r, m, n, p, k = UNITS[name]
+        _, _, rows, _ = area(name)
+        u = ORDER.index(name)
+        for copy in x_copy(name):
+            copy.wait_recv()
+        wide = k * part // 2
+        for i, more in enumerate(unsqueeze(xin[u, : n * ry, :wide], xin_step[u])):
+            lanes = pl.ds(p * part + i * wide, wide)
+            done[kind, r, rows, lanes] = gram[kind, r, my_y, my_x, rows, lanes] + more
 
     def onehots(r):
         seg_t = (segn if r == 3 else tseg_ref)[...]
@@ -334,12 +395,23 @@
             qa_arrival(m, far).wait_recv()
         qa_hop(m).start()
 
+    for j in range(4):
+        local(j).start()
+    greet = [sibling, x_peer, x_other]
+    greet += [(up, spot(my_y, my_x, other)), (down, spot(my_y, my_x, other))]
+    greet += [y_peer(d) for d in range(1, NY)]
+    greet += [y_peer(d, up) for d in range(NY)]
+    greet += [y_peer(d, down) for d in range(NY)]
+    barrier = pltpu.get_barrier_semaphore()
+    for who in greet:
+        pl.semaphore_signal(barrier, inc=1, device_id=who, device_id_type=MESH)
+    pl.semaphore_wait(barrier, len(greet))
+
     for far in range(2):
         qg_up(far).start()
     tg_down(0).start()
     for j in range(4):
         swap_out(j).start()
-        local(j).start()
     for far in range(2):
         qa_up(0, far).start()
     ta_down(0).start()
@@ -485,8 +557,10 @@
         g_move(r).wait_send()
     for name in ORDER:
         for d in range(1, NY):
-            y_copy(name, d).wait_send()
-        x_copy(name).wait_send()
+            for copy in y_copy(name, d):
+                copy.wait_send()
+        for copy in x_copy(name):
+            copy.wait_send()
 
 
 def on_device(n_doc, train_acts, train_grads, query_acts, query_grads, train_seg, query_seg):
@@ -514,8 +588,14 @@
             pltpu.VMEM((3, half, NCORE * wide_a), bf16),
             pltpu.VMEM((2, half, NCORE * wide_g), bf16),
             pltpu.VMEM((2, CYCLE, NY, NX, rows, rows_t), F32),
-            pltpu.VMEM((2, CYCLE, NY - 1, NX, rows, rows_t), F32),
-            pltpu.VMEM((2, CYCLE, rows, rows_t), F32),
+            pltpu.VMEM((2, CYCLE, NY, rows, rows_t), I32),
+            pltpu.VMEM((units, NY, 8, LANES), F32),
+            pltpu.VMEM((2, CYCLE, NY - 1, rows, rows_t), I32),
+            pltpu.VMEM((units, NY - 1, 8, LANES), F32),
+            pltpu.VMEM((units, rows, rows_t // 2), I32),
+            pltpu.VMEM((units, 8, LANES), F32),
+            pltpu.VMEM((units, rows, rows_t // 2), I32),
+            pltpu.VMEM((units, 8, LANES), F32),
             pltpu.VMEM((2, CYCLE, rows, rows_t), F32),
             pltpu.VMEM((2, rows, rows_t), F32),
             pltpu.VMEM((1, rows_t), jnp.int32),
@@ -531,8 +611,8 @@
             *pair(TPARTS),
             *pair(2),
             *pair(TPARTS),
-            *pair(units, NY - 1),
-            *pair(units),
+            *pair(units, NY - 1, 2),
+            *pair(units, 2),
             *pair(2),
             dma,
             dma,

time: 158 us -> 153 us (0.968)
  Pallas kernels: 156 us -> 152 us
    pallas_call x1, Pallas kernels: 156 us -> 152 us  [on_device(): pl.pallas_call(functools.partial(kernel, n_doc), out_shape=jax.ShapeDtype...]
where the time goes in v4:
time: 153 us
  Pallas kernels  152 us (99%)
    pallas_call x1, Pallas kernels, on_device(): pl.pallas_call(functools.partial(kernel, n_doc), out_shape=jax.ShapeDtype...  152 us

profile of v4, /device:TPU:1, one launch (start us, length us, event | category | flops | bytes accessed | tf_op | source)
XLA Modules:
  0.0 153.3 jit_solution(11895115522348252164)
XLA Ops:
  0.0 152.0 %influence.1 = f32[8,32]{1,0:T(8,128)} custom-call(bf16[768,1792]{1,0:T(8,128)(2,1)} %ta_hbm.1, bf16[768,512]{1,0:T(8,128)(2,1)} %tg_hbm.1, bf16[512,1792]{1,0:T(8,128)(2,1)} %qa_hbm.1, bf16[512,512]{1,0:T(8,128)(2,1)} %qg_hbm.1, s32[1,768]{1,0:T(1,128)} %tseg_ref.1, s32[16,512]{1,0:T(8,128)} %qseg_ref.1), custom_call_target="tpu_custom_call" | custom-call | tf_op jit(solution)/shard_map/influence/pallas_call | solution.py:580
  152.0 1.3 copy.8

commit v5 on v4

--- a/solution.py
+++ b/solution.py
@@ -14,6 +14,7 @@
 NY = 4
 NX = 2
 NCORE = 2
+X_HI = 2
 CHUNKS = 4
 TPARTS = 3
 LANES = 128
@@ -40,8 +41,8 @@
     "a2_3": (ACT, 2, 3, 1, 0, 3),
     "a3_01": (ACT, 3, 0, 2, 0, 2),
     "a3_2": (ACT, 3, 2, 1, 0, 2),
-    "a3_3": (ACT, 3, 3, 1, 0, 2),
-    "a3_all": (ACT, 3, 0, 4, 2, 1),
+    "a3_3": (ACT, 3, 3, 1, 0, 3),
+    "a3_last": (ACT, 3, 0, 3, 2, 1),
 }
 ORDER = list(UNITS)
 
@@ -96,7 +97,11 @@
     xin,
     xin_step,
     done,
+    gout,
+    gout_step,
     gin,
+    gin_step,
+    grads_up,
     segn,
     small,
     fin_y,
@@ -155,6 +160,13 @@
         return y * (NX * NCORE) + x * NCORE + c
 
     sibling = (doc, spot(my_y, my_x, other))
+    deep = n_doc // X_HI
+    wrap = lax.rem(doc, deep) // (deep - 1)
+    keep_far = my_x + wrap * (1 - 2 * my_x)
+
+    def keep(kind, r):
+        return keep_far if kind == GRAD and r >= 2 else my_x
+
     x_peer = (doc, spot(my_y, 1 - my_x, core))
     x_other = (doc, spot(my_y, 1 - my_x, other))
 
@@ -326,8 +338,12 @@
             remote(xout_step.at[u], xin_step.at[u], x_send.at[u, 1], x_recv.at[u, 1], x_peer),
         )
 
-    def g_move(r):
-        return remote(done.at[GRAD, r], gin.at[r - 2], g_send.at[r - 2], g_recv.at[r - 2], (up, place))
+    def g_move():
+        who = (up, spot(my_y, keep_far, core))
+        return (
+            remote(gout, gin, g_send.at[0], g_recv.at[0], who),
+            remote(gout_step, gin_step, g_send.at[1], g_recv.at[1], who),
+        )
 
     def unit(name):
         compute(name)
@@ -347,7 +363,7 @@
             high, low = high + more[0], low + more[1]
         gram[kind, r, my_y, 0, rows, lanes] = high
         gram[kind, r, my_y, 1, rows, lanes] = low
-        go = gram[kind, r, my_y, 1 - my_x, rows, lanes]
+        go = gram[kind, r, my_y, 1 - keep(kind, r), rows, lanes]
         wide = k * part // 2
         packed, step = squeeze(go[:, :wide], go[:, wide:])
         xout[u, : n * ry, :wide] = packed
@@ -364,7 +380,7 @@
         wide = k * part // 2
         for i, more in enumerate(unsqueeze(xin[u, : n * ry, :wide], xin_step[u])):
             lanes = pl.ds(p * part + i * wide, wide)
-            done[kind, r, rows, lanes] = gram[kind, r, my_y, my_x, rows, lanes] + more
+            done[kind, r, rows, lanes] = gram[kind, r, my_y, keep(kind, r), rows, lanes] + more
 
     def onehots(r):
         seg_t = (segn if r == 3 else tseg_ref)[...]
@@ -380,7 +396,7 @@
 
     def segment_sum(r, hots):
         onehot_t, onehot_q = hots
-        grads = gin[r - 2] if r >= 2 else done[GRAD, r]
+        grads = grads_up[r - 2] if r >= 2 else done[GRAD, r]
         left = lax.dot_general(
             onehot_t,
             done[ACT, r] * grads,
@@ -399,6 +415,7 @@
         local(j).start()
     greet = [sibling, x_peer, x_other]
     greet += [(up, spot(my_y, my_x, other)), (down, spot(my_y, my_x, other))]
+    greet += [(up, spot(my_y, 1 - my_x, core)), (down, spot(my_y, 1 - my_x, core))]
     greet += [y_peer(d) for d in range(1, NY)]
     greet += [y_peer(d, up) for d in range(NY)]
     greet += [y_peer(d, down) for d in range(NY)]
@@ -461,9 +478,6 @@
     qa_hop(1).wait_recv()
     unit("a2_1")
     y_finish("g3")
-    for name in ("g0", "a0", "g1", "g2"):
-        x_finish(name)
-    g_move(2).start()
     y_finish("a2_0")
     ta_down(1).wait_recv()
     ta_across(1, core).start()
@@ -471,34 +485,46 @@
         ta_across(p, other).wait_recv()
     unit("a3_01")
     y_finish("a2_1")
-    for name in ("a1_01", "a1_23", "g3"):
-        x_finish(name)
-    g_move(3).start()
-    base = segment_sum(0, onehots(0)) + segment_sum(1, onehots(1))
     seg_copy.wait_recv()
     hots_2, hots_3 = onehots(2), onehots(3)
     qa_hop(2).wait_recv()
     unit("a2_2")
     unit("a3_2")
     y_finish("a3_01")
-    for name in ("a2_0", "a2_1"):
-        x_finish(name)
     y_finish("a2_2")
     y_finish("a3_2")
     ta_down(2).wait_recv()
     ta_across(2, core).start()
+    for name in ("g2", "g3"):
+        x_finish(name)
+    gout[...], gout_step[...] = squeeze(done[GRAD, 2], done[GRAD, 3])
+    for copy in g_move():
+        copy.start()
+    ta_across(2, other).wait_recv()
+    unit("a3_last")
     qa_hop(3).wait_recv()
     unit("a3_3")
     unit("a2_3")
-    ta_across(2, other).wait_recv()
-    unit("a3_all")
-    for name in ("a3_01", "a2_2", "a3_2"):
+    for name in ("g0", "a0", "g1", "a1_01", "a1_23"):
         x_finish(name)
+    base = segment_sum(0, onehots(0)) + segment_sum(1, onehots(1))
+    for name in ("a2_0", "a2_1", "a3_01", "a2_2", "a3_2"):
+        x_finish(name)
+    y_finish("a3_last")
     y_finish("a3_3")
     y_finish("a2_3")
-    y_finish("a3_all")
-    for r in range(2, CYCLE):
-        g_move(r).wait_recv()
+    for copy in g_move():
+        copy.wait_recv()
+    grads_up[0], grads_up[1] = unsqueeze(gin[...], gin_step[...])
+    x_finish("a3_last")
+    x_finish("a3_3")
+    small[...] = segment_sum(3, hots_3)
+    fu = [
+        remote(small, fin_y.at[1, my_y], fy_send.at[1, d], fy_recv.at[1, my_y], y_peer(d, up))
+        for d in range(NY)
+    ]
+    for copy in fu:
+        copy.start()
     x_finish("a2_3")
     fin_y[0, my_y] = base + segment_sum(2, hots_2)
     fy = [
@@ -506,15 +532,6 @@
         for d in range(1, NY)
     ]
     for copy in fy:
-        copy.start()
-    x_finish("a3_3")
-    x_finish("a3_all")
-    small[...] = segment_sum(3, hots_3)
-    fu = [
-        remote(small, fin_y.at[1, my_y], fy_send.at[1, d], fy_recv.at[1, my_y], y_peer(d, up))
-        for d in range(NY)
-    ]
-    for copy in fu:
         copy.start()
     for d in range(1, NY):
         y = y_of(d)
@@ -553,8 +570,8 @@
     for p in range(TPARTS):
         ta_down(p).wait_send()
         ta_across(p, core).wait_send()
-    for r in range(2, CYCLE):
-        g_move(r).wait_send()
+    for copy in g_move():
+        copy.wait_send()
     for name in ORDER:
         for d in range(1, NY):
             for copy in y_copy(name, d):
@@ -597,8 +614,12 @@
             pltpu.VMEM((units, rows, rows_t // 2), I32),
             pltpu.VMEM((units, 8, LANES), F32),
             pltpu.VMEM((2, CYCLE, rows, rows_t), F32),
+            pltpu.VMEM((rows, rows_t), I32),
+            pltpu.VMEM((8, LANES), F32),
+            pltpu.VMEM((rows, rows_t), I32),
+            pltpu.VMEM((8, LANES), F32),
             pltpu.VMEM((2, rows, rows_t), F32),
-            pltpu.VMEM((1, rows_t), jnp.int32),
+            pltpu.VMEM((1, rows_t), I32),
             pltpu.VMEM((ST, LANES), F32),
             pltpu.VMEM((2, NY, ST, LANES), F32),
             pltpu.VMEM((NX * NCORE, ST, LANES), F32),

time: 153 us -> 140 us (0.915)
  Pallas kernels: 152 us -> 138 us
    pallas_call x1, Pallas kernels: 152 us -> 138 us  [on_device(): pl.pallas_call(functools.partial(kernel, n_doc), out_shape=jax.ShapeDtype...]
where the time goes in v5:
time: 140 us
  Pallas kernels  138 us (99%)
    pallas_call x1, Pallas kernels, on_device(): pl.pallas_call(functools.partial(kernel, n_doc), out_shape=jax.ShapeDtype...  138 us

profile of v5, /device:TPU:1, one launch (start us, length us, event | category | flops | bytes accessed | tf_op | source)
XLA Modules:
  0.0 139.7 jit_solution(13815232988876498211)
XLA Ops:
  0.0 138.4 %influence.1 = f32[8,32]{1,0:T(8,128)} custom-call(bf16[768,1792]{1,0:T(8,128)(2,1)} %ta_hbm.1, bf16[768,512]{1,0:T(8,128)(2,1)} %tg_hbm.1, bf16[512,1792]{1,0:T(8,128)(2,1)} %qa_hbm.1, bf16[512,512]{1,0:T(8,128)(2,1)} %qg_hbm.1, s32[1,768]{1,0:T(1,128)} %tseg_ref.1, s32[16,512]{1,0:T(8,128)} %qseg_ref.1), custom_call_target="tpu_custom_call" | custom-call | tf_op jit(solution)/shard_map/influence/pallas_call | solution.py:597
  138.4 1.3 copy.8

commit v6 on v5

--- a/solution.py
+++ b/solution.py
@@ -45,6 +45,7 @@
     "a3_last": (ACT, 3, 0, 3, 2, 1),
 }
 ORDER = list(UNITS)
+HELD = ("g0", "a0", "g1", "a1_01", "a1_23")
 
 
 def spread(tile, rows, lanes):
@@ -72,6 +73,14 @@
     low = packed - high * 65536
     step = spread(step, *packed.shape)
     return high.astype(F32) * step, low.astype(F32) * step
+
+
+def thirds(value, axis):
+    parts = []
+    for _ in range(3):
+        parts.append(value.astype(jnp.bfloat16))
+        value = value - parts[-1].astype(F32)
+    return jnp.concatenate(parts, axis=axis)
 
 
 def kernel(
@@ -106,6 +115,7 @@
     small,
     fin_y,
     fin_x,
+    early_sum,
     local_sem,
     own_send,
     own_recv,
@@ -245,10 +255,19 @@
             (up, spot(my_y, my_x, who_up(far))),
         )
 
-    def qa_hop(m):
+    def qa_hop(m, far):
+        at = cols(wide_a, who_up(far))
         return remote(
-            qa.at[1, q_chunk(m), :], qa.at[2, q_chunk(m), :], hop_send.at[m], hop_recv.at[m], (up, place)
-        )
+            qa.at[1, q_chunk(m), at],
+            qa.at[2, q_chunk(m), at],
+            hop_send.at[m, far],
+            hop_recv.at[m, far],
+            (up, place),
+        )
+
+    def hop_arrival(m):
+        for far in range(2):
+            qa_hop(m, far).wait_recv()
 
     def tg_down(step):
         src = tg_hbm if step == 0 else tg.at[step, :, cols(wide_g, core)]
@@ -281,6 +300,19 @@
     def area(name):
         kind, r, m, n, p, k = UNITS[name]
         return kind, r, pl.ds(m * ry, n * ry), pl.ds(p * part, k * part)
+
+    early = []
+
+    def half_compute(name):
+        _, r, m, n, _, _ = UNITS[name]
+        at = cols(wide_a, core)
+        early_sum[len(early)] = lax.dot_general(
+            ta[1 if r == 3 else 0, :, at],
+            qa[2, m * chunk : (m + n) * chunk, at],
+            CONTRACT,
+            preferred_element_type=F32,
+        )
+        early.append(name)
 
     def compute(name):
         kind, r, m, n, p, k = UNITS[name]
@@ -290,7 +322,16 @@
             query, train = qg.at[min(r, 1)], tg.at[max(r - 1, 0)]
         left = query[m * chunk : (m + n) * chunk, :]
         right = train[p * part : (p + k) * part, :]
-        if n == CHUNKS:
+        if name in early:
+            at = cols(wide_a, other)
+            late = lax.dot_general(
+                ta[1 if r == 3 else 0, :, at],
+                qa[2, m * chunk : (m + n) * chunk, at],
+                CONTRACT,
+                preferred_element_type=F32,
+            )
+            total = (early_sum[early.index(name)] + late).T
+        elif n == CHUNKS:
             total = lax.dot_general(left, right, CONTRACT, preferred_element_type=F32)
         else:
             total = lax.dot_general(right, left, CONTRACT, preferred_element_type=F32).T
@@ -351,6 +392,10 @@
             for copy in y_copy(name, d):
                 copy.start()
 
+    def x_start(name):
+        for copy in x_copy(name):
+            copy.start()
+
     def y_finish(name):
         kind, r, m, n, p, k = UNITS[name]
         _, _, rows, lanes = area(name)
@@ -368,8 +413,8 @@
         packed, step = squeeze(go[:, :wide], go[:, wide:])
         xout[u, : n * ry, :wide] = packed
         xout_step[u] = step
-        for copy in x_copy(name):
-            copy.start()
+        if name not in HELD:
+            x_start(name)
 
     def x_finish(name):
         kind, r, m, n, p, k = UNITS[name]
@@ -384,7 +429,7 @@
 
     def onehots(r):
         seg_t = (segn if r == 3 else tseg_ref)[...]
-        onehot_t = (lax.broadcasted_iota(jnp.int32, (ST, rows_t), 0) == seg_t).astype(F32)
+        onehot_t = (lax.broadcasted_iota(jnp.int32, (ST, rows_t), 0) == seg_t).astype(jnp.bfloat16)
         owner = lax.rem(doc + n_doc - min(r, 2), n_doc)
         seg_q = qseg_ref[pl.ds(owner, 1), :]
         row = lax.broadcasted_iota(jnp.int32, (CHUNKS * ry, rows_q), 0)
@@ -392,24 +437,21 @@
         mine = core * half + (row // ry) * chunk + my_y * (NX * ry) + my_x * ry + row % ry
         ids = jnp.sum(jnp.where(token == mine, seg_q, 0), axis=1, keepdims=True)
         lane = lax.broadcasted_iota(jnp.int32, (CHUNKS * ry, LANES), 1)
-        return onehot_t, (lane == ids + r * SQ).astype(F32)
+        onehot_q = (lane == ids + r * SQ).astype(jnp.bfloat16)
+        return onehot_t, jnp.concatenate([onehot_q] * 3, axis=0)
 
     def segment_sum(r, hots):
         onehot_t, onehot_q = hots
         grads = grads_up[r - 2] if r >= 2 else done[GRAD, r]
-        left = lax.dot_general(
-            onehot_t,
-            done[ACT, r] * grads,
-            CONTRACT,
-            precision=lax.Precision.HIGHEST,
-            preferred_element_type=F32,
-        )
-        return jnp.dot(left, onehot_q, precision=lax.Precision.HIGHEST, preferred_element_type=F32)
+        parts = thirds(done[ACT, r] * grads, 0)
+        left = lax.dot_general(onehot_t, parts, CONTRACT, preferred_element_type=F32)
+        total = jnp.dot(thirds(left, 0), onehot_q, preferred_element_type=F32)
+        return (total[:ST] + total[ST : 2 * ST]) + total[2 * ST :]
 
     def arrive_and_hop(m):
         for far in range(2):
             qa_arrival(m, far).wait_recv()
-        qa_hop(m).start()
+            qa_hop(m, far).start()
 
     for j in range(4):
         local(j).start()
@@ -472,10 +514,10 @@
     y_finish("a1_01")
     tg_across(1, other).wait_recv()
     unit("g3")
-    qa_hop(0).wait_recv()
+    hop_arrival(0)
     unit("a2_0")
     y_finish("a1_23")
-    qa_hop(1).wait_recv()
+    hop_arrival(1)
     unit("a2_1")
     y_finish("g3")
     y_finish("a2_0")
@@ -486,8 +528,8 @@
     unit("a3_01")
     y_finish("a2_1")
     seg_copy.wait_recv()
-    hots_2, hots_3 = onehots(2), onehots(3)
-    qa_hop(2).wait_recv()
+    hots_0, hots_1, hots_2, hots_3 = onehots(0), onehots(1), onehots(2), onehots(3)
+    hop_arrival(2)
     unit("a2_2")
     unit("a3_2")
     y_finish("a3_01")
@@ -502,17 +544,22 @@
         copy.start()
     ta_across(2, other).wait_recv()
     unit("a3_last")
-    qa_hop(3).wait_recv()
+    qa_hop(3, 0).wait_recv()
+    for name in ("a3_3", "a2_3"):
+        half_compute(name)
+    qa_hop(3, 1).wait_recv()
+    for name in HELD:
+        x_start(name)
     unit("a3_3")
     unit("a2_3")
-    for name in ("g0", "a0", "g1", "a1_01", "a1_23"):
-        x_finish(name)
-    base = segment_sum(0, onehots(0)) + segment_sum(1, onehots(1))
     for name in ("a2_0", "a2_1", "a3_01", "a2_2", "a3_2"):
         x_finish(name)
     y_finish("a3_last")
     y_finish("a3_3")
     y_finish("a2_3")
+    for name in HELD:
+        x_finish(name)
+    base = segment_sum(0, hots_0) + segment_sum(1, hots_1)
     for copy in g_move():
         copy.wait_recv()
     grads_up[0], grads_up[1] = unsqueeze(gin[...], gin_step[...])
@@ -563,7 +610,7 @@
     for m in range(CHUNKS):
         for far in range(2):
             qa_up(m, far).wait_send()
-        qa_hop(m).wait_send()
+            qa_hop(m, far).wait_send()
     for step in range(2):
         tg_down(step).wait_send()
         tg_across(step, core).wait_send()
@@ -623,11 +670,12 @@
             pltpu.VMEM((ST, LANES), F32),
             pltpu.VMEM((2, NY, ST, LANES), F32),
             pltpu.VMEM((NX * NCORE, ST, LANES), F32),
+            pltpu.VMEM((2, rows_t, half // CHUNKS), F32),
             dma((4,)),
             *pair(4),
             *pair(2),
             *pair(CHUNKS, 2),
-            *pair(CHUNKS),
+            *pair(CHUNKS, 2),
             *pair(2),
             *pair(TPARTS),
             *pair(2),

time: 140 us -> 135 us (0.964)
  Pallas kernels: 138 us -> 133 us
    pallas_call x1, Pallas kernels: 138 us -> 133 us  [on_device(): pl.pallas_call(functools.partial(kernel, n_doc), out_shape=jax.ShapeDtype...]
where the time goes in v6:
time: 135 us
  Pallas kernels  133 us (99%)
    pallas_call x1, Pallas kernels, on_device(): pl.pallas_call(functools.partial(kernel, n_doc), out_shape=jax.ShapeDtype...  133 us

profile of v6, /device:TPU:1, one launch (start us, length us, event | category | flops | bytes accessed | tf_op | source)
XLA Modules:
  0.0 134.7 jit_solution(4358258147767165746)
XLA Ops:
  0.0 133.4 %influence.1 = f32[8,32]{1,0:T(8,128)} custom-call(bf16[768,1792]{1,0:T(8,128)(2,1)} %ta_hbm.1, bf16[768,512]{1,0:T(8,128)(2,1)} %tg_hbm.1, bf16[512,1792]{1,0:T(8,128)(2,1)} %qa_hbm.1, bf16[512,512]{1,0:T(8,128)(2,1)} %qg_hbm.1, s32[1,768]{1,0:T(1,128)} %tseg_ref.1, s32[16,512]{1,0:T(8,128)} %qseg_ref.1), custom_call_target="tpu_custom_call" | custom-call | tf_op jit(solution)/shard_map/influence/pallas_call | solution.py:644
  133.4 1.3 copy.8

commit v7 on v6

--- a/solution.py
+++ b/solution.py
@@ -339,16 +339,6 @@
             gram[kind, r, :, :, (m + i) * ry : (m + i + 1) * ry, p * part : (p + k) * part] = total[
                 i * chunk : (i + 1) * chunk
             ].reshape(NY, NX, ry, k * part)
-        u = ORDER.index(name)
-        _, _, rows, lanes = area(name)
-
-        def code(y, carry):
-            packed, step = squeeze(gram[kind, r, y, 0, rows, lanes], gram[kind, r, y, 1, rows, lanes])
-            yout[kind, r, y, rows, lanes] = packed
-            yout_step[u, y] = step
-            return carry
-
-        lax.fori_loop(0, NY, code, 0)
 
     def y_copy(name, d):
         kind, r, rows, lanes = area(name)
@@ -388,7 +378,12 @@
 
     def unit(name):
         compute(name)
+        kind, r, rows, lanes = area(name)
         for d in range(1, NY):
+            y = y_of(d)
+            packed, step = squeeze(gram[kind, r, y, 0, rows, lanes], gram[kind, r, y, 1, rows, lanes])
+            yout[kind, r, y, rows, lanes] = packed
+            yout_step[ORDER.index(name), y] = step
             for copy in y_copy(name, d):
                 copy.start()
 
@@ -537,11 +532,6 @@
     y_finish("a3_2")
     ta_down(2).wait_recv()
     ta_across(2, core).start()
-    for name in ("g2", "g3"):
-        x_finish(name)
-    gout[...], gout_step[...] = squeeze(done[GRAD, 2], done[GRAD, 3])
-    for copy in g_move():
-        copy.start()
     ta_across(2, other).wait_recv()
     unit("a3_last")
     qa_hop(3, 0).wait_recv()
@@ -552,6 +542,11 @@
         x_start(name)
     unit("a3_3")
     unit("a2_3")
+    for name in ("g2", "g3"):
+        x_finish(name)
+    gout[...], gout_step[...] = squeeze(done[GRAD, 2], done[GRAD, 3])
+    for copy in g_move():
+        copy.start()
     for name in ("a2_0", "a2_1", "a3_01", "a2_2", "a3_2"):
         x_finish(name)
     y_finish("a3_last")

time: 135 us -> 134 us (level)
  no operation moved by 1% of the time
where the time goes in v7:
time: 134 us
  Pallas kernels  133 us (99%)
    pallas_call x1, Pallas kernels, on_device(): pl.pallas_call(functools.partial(kernel, n_doc), out_shape=jax.ShapeDtype...  133 us

profile of v7, /device:TPU:1, one launch (start us, length us, event | category | flops | bytes accessed | tf_op | source)
XLA Modules:
  0.0 133.9 jit_solution(3985165512059262874)
XLA Ops:
  0.0 132.6 %influence.1 = f32[8,32]{1,0:T(8,128)} custom-call(bf16[768,1792]{1,0:T(8,128)(2,1)} %ta_hbm.1, bf16[768,512]{1,0:T(8,128)(2,1)} %tg_hbm.1, bf16[512,1792]{1,0:T(8,128)(2,1)} %qa_hbm.1, bf16[512,512]{1,0:T(8,128)(2,1)} %qg_hbm.1, s32[1,768]{1,0:T(1,128)} %tseg_ref.1, s32[16,512]{1,0:T(8,128)} %qseg_ref.1), custom_call_target="tpu_custom_call" | custom-call | tf_op jit(solution)/shard_map/influence/pallas_call | solution.py:639
  132.6 1.3 copy.8

commit v8 on v7

--- a/solution.py
+++ b/solution.py
@@ -542,6 +542,7 @@
         x_start(name)
     unit("a3_3")
     unit("a2_3")
+    y_finish("a3_last")
     for name in ("g2", "g3"):
         x_finish(name)
     gout[...], gout_step[...] = squeeze(done[GRAD, 2], done[GRAD, 3])
@@ -549,7 +550,6 @@
         copy.start()
     for name in ("a2_0", "a2_1", "a3_01", "a2_2", "a3_2"):
         x_finish(name)
-    y_finish("a3_last")
     y_finish("a3_3")
     y_finish("a2_3")
     for name in HELD:

time: 134 us -> 134 us (level)
  no operation moved by 1% of the time
where the time goes in v8:
time: 134 us
  Pallas kernels  133 us (99%)
    pallas_call x1, Pallas kernels, on_device(): pl.pallas_call(functools.partial(kernel, n_doc), out_shape=jax.ShapeDtype...  133 us

profile of v8, /device:TPU:1, one launch (start us, length us, event | category | flops | bytes accessed | tf_op | source)
XLA Modules:
  0.0 133.9 jit_solution(2397087873788961073)
XLA Ops:
  0.0 132.6 %influence.1 = f32[8,32]{1,0:T(8,128)} custom-call(bf16[768,1792]{1,0:T(8,128)(2,1)} %ta_hbm.1, bf16[768,512]{1,0:T(8,128)(2,1)} %tg_hbm.1, bf16[512,1792]{1,0:T(8,128)(2,1)} %qa_hbm.1, bf16[512,512]{1,0:T(8,128)(2,1)} %qg_hbm.1, s32[1,768]{1,0:T(1,128)} %tseg_ref.1, s32[16,512]{1,0:T(8,128)} %qseg_ref.1), custom_call_target="tpu_custom_call" | custom-call | tf_op jit(solution)/shard_map/influence/pallas_call | solution.py:639
  132.6 1.3 copy.8

commit v9 on v7

--- a/solution.py
+++ b/solution.py
@@ -593,7 +593,7 @@
     for i, (x, c) in enumerate(((my_x, other), (1 - my_x, core), (1 - my_x, other))):
         at = x * NCORE + c
         remote(fin_x.at[at], fin_x.at[at], fx_send.at[i], fx_recv.at[at], sibling).wait_recv()
-    out_ref[...] = (((fin_x[0] + fin_x[1]) + (fin_x[2] + fin_x[3])) * factor)[:, : CYCLE * SQ]
+    out_ref[...] = ((fin_x[0] + fin_x[1]) + (fin_x[2] + fin_x[3])) * factor
 
     seg_copy.wait_send()
     for copy in fy + fu + fx:
@@ -636,9 +636,9 @@
     def pair(*shape):
         return [dma(shape), dma(shape)]
 
-    return pl.pallas_call(
+    sums = pl.pallas_call(
         functools.partial(kernel, n_doc),
-        out_shape=jax.ShapeDtypeStruct((ST, CYCLE * SQ), F32),
+        out_shape=jax.ShapeDtypeStruct((ST, LANES), F32),
         in_specs=[anywhere] * 4 + [vmem] * 2,
         out_specs=vmem,
         scratch_shapes=[
@@ -688,6 +688,7 @@
         ),
         name="influence",
     )(train_acts, train_grads, query_acts, query_grads, train_seg, query_seg)
+    return sums[:, : CYCLE * SQ]
 
 
 def solution(mesh):

time: 134 us -> 134 us (level)
  no operation moved by 1% of the time
where the time goes in v9:
time: 134 us
  Pallas kernels  133 us (99%)
    pallas_call x1, Pallas kernels, on_device(): pl.pallas_call(functools.partial(kernel, n_doc), out_shape=jax.ShapeDtype...  133 us

profile of v9, /device:TPU:1, one launch (start us, length us, event | category | flops | bytes accessed | tf_op | source)
XLA Modules:
  0.0 133.9 jit_solution(12522013421544282365)
XLA Ops:
  0.0 132.6 %influence.1 = f32[8,128]{1,0:T(8,128)} custom-call(bf16[768,1792]{1,0:T(8,128)(2,1)} %ta_hbm.1, bf16[768,512]{1,0:T(8,128)(2,1)} %tg_hbm.1, bf16[512,1792]{1,0:T(8,128)(2,1)} %qa_hbm.1, bf16[512,512]{1,0:T(8,128)(2,1)} %qg_hbm.1, s32[1,768]{1,0:T(1,128)} %tseg_ref.1, s32[16,512]{1,0:T(8,128)} %qseg_ref.1), custom_call_target="tpu_custom_call" | custom-call | tf_op jit(solution)/shard_map/influence/pallas_call | solution.py:639
  132.6 1.3 copy.8

commit v10 on v7

--- a/solution.py
+++ b/solution.py
@@ -450,12 +450,12 @@
 
     for j in range(4):
         local(j).start()
-    greet = [sibling, x_peer, x_other]
+    greet = [y_peer(d, up) for d in range(NY)]
+    greet += [y_peer(d, down) for d in range(NY)]
     greet += [(up, spot(my_y, my_x, other)), (down, spot(my_y, my_x, other))]
     greet += [(up, spot(my_y, 1 - my_x, core)), (down, spot(my_y, 1 - my_x, core))]
     greet += [y_peer(d) for d in range(1, NY)]
-    greet += [y_peer(d, up) for d in range(NY)]
-    greet += [y_peer(d, down) for d in range(NY)]
+    greet += [x_peer, x_other, sibling]
     barrier = pltpu.get_barrier_semaphore()
     for who in greet:
         pl.semaphore_signal(barrier, inc=1, device_id=who, device_id_type=MESH)

time: 134 us -> 134 us (level)
  no operation moved by 1% of the time
where the time goes in v10:
time: 134 us
  Pallas kernels  133 us (99%)
    pallas_call x1, Pallas kernels, on_device(): pl.pallas_call(functools.partial(kernel, n_doc), out_shape=jax.ShapeDtype...  133 us

profile of v10, /device:TPU:1, one launch (start us, length us, event | category | flops | bytes accessed | tf_op | source)
XLA Modules:
  0.0 133.9 jit_solution(1009918292700578961)
XLA Ops:
  0.0 132.6 %influence.1 = f32[8,32]{1,0:T(8,128)} custom-call(bf16[768,1792]{1,0:T(8,128)(2,1)} %ta_hbm.1, bf16[768,512]{1,0:T(8,128)(2,1)} %tg_hbm.1, bf16[512,1792]{1,0:T(8,128)(2,1)} %qa_hbm.1, bf16[512,512]{1,0:T(8,128)(2,1)} %qg_hbm.1, s32[1,768]{1,0:T(1,128)} %tseg_ref.1, s32[16,512]{1,0:T(8,128)} %qseg_ref.1), custom_call_target="tpu_custom_call" | custom-call | tf_op jit(solution)/shard_map/influence/pallas_call | solution.py:639
  132.6 1.3 copy.8
